TPU v7x, 256 devices: a whole 4x4x8 slice. The times are simulated.
256 devices in a mesh: dp: 8 (over x, y_lo), section: 2 (over core), mp: 16 (over z, y_hi).
Axes of the slice: x: 4, y: 4 (y_hi: 2, y_lo: 2; y = y_hi * 2 + y_lo), z: 8, core: 2. Of those that a mesh axis runs over, the one named last changes fastest.
Arguments:
- features: bfloat16 [3, 128, 8192], P(None, 'dp', ('section', 'mp')), may hold values from -6 to 6
- fc_weight: bfloat16 [3, 8192, 8192], P(None, ('section', 'mp'), 'dp'), may hold values from -0.0390625 to 0.0390625
- head: bfloat16 [128256, 8192], P(('dp', 'section', 'mp')), may hold values from -8 to 8, as said below
- draft_gain: float32 [8192], P('dp'), may hold values from 0.1 to 1.9
- target_gain: float32 [8192], P(('section', 'mp')), may hold values from 0.1 to 1.9
- teacher_index: int32 [128, 32], replicated, may hold values from 0 to 128255, as said below
Outputs:
- weight_grad: bfloat16 [3, 8192, 8192], P(None, ('section', 'mp'), 'dp')
- gain_grad: float32 [8192], P('dp')
- token_loss: float32 [128], P('dp')
Inputs may be any that keep to these rules, and one draw needn't show every extreme that they name: `teacher_index`: the 32 entries of a row are distinct. `head`: each row is a normal of scale 3 / sqrt(8192), truncated at six scales, times a factor of the row between 1 and 40, clipped to the range.
All inputs are finite; a program needn't handle non-finite values.
Results may differ from a plain program's by a relative error of at most 0.012.
The roundings to bfloat16 on the way count: a program that leaves them out, or rounds other values in their place, can miss the bound.
Values may be sent and summed in bfloat16 or wider, within the bound.
A program may use at most 192 MiB of HBM per device.

v0:
```python
import jax
import jax.numpy as jnp
from jax import lax
from jax.sharding import PartitionSpec as P

D = 8192


norm_eps = 1e-05


def shards(features, fc_weight, head, draft_gain, target_gain, teacher_index):
    rows_dp = features.shape[1]
    gathered = lax.all_gather(features, "dp", axis=1, tiled=True)
    total_rows = gathered.shape[1]
    vocab_rows = head.shape[0]
    tok_rows = gathered
    joined = lax.psum_scatter(
        jnp.einsum("jtf,jfc->tc", tok_rows, fc_weight, preferred_element_type=jnp.float32),
        ("section", "mp"),
        scatter_dimension=0,
        tiled=True,
    )
    square_sum = lax.psum(jnp.sum(joined * joined, axis=1), "dp")
    draft_scale = lax.rsqrt(square_sum / D + norm_eps)
    normed = (joined * draft_scale[:, None] * draft_gain[None, :]).astype(jnp.bfloat16)
    high_state = gathered[2].astype(jnp.float32)
    target_sum = lax.psum(jnp.sum(high_state * high_state, axis=1), ("section", "mp"))
    target_scale = lax.rsqrt(target_sum / D + norm_eps)
    teacher_in = (high_state * target_scale[:, None] * target_gain[None, :]).astype(jnp.bfloat16)
    dims = (((1,), (1,)), ((), ()))
    teacher_logits = lax.dot_general(
        lax.all_gather(teacher_in, ("section", "mp"), axis=1, tiled=True),
        head,
        dims,
        preferred_element_type=jnp.float32,
    )
    wide_rows = lax.all_gather(normed, "dp", axis=1, tiled=True)
    draft_logits = lax.dot_general(
        lax.all_gather(wide_rows, ("section", "mp"), axis=0, tiled=True),
        head,
        dims,
        preferred_element_type=jnp.float32,
    )
    vocab_start = lax.axis_index(("dp", "section", "mp")) * vocab_rows
    local_index = teacher_index - vocab_start
    inside = (local_index >= 0) & (local_index < vocab_rows)
    clipped = jnp.clip(local_index, 0, vocab_rows - 1)
    teacher_local = jnp.where(inside, jnp.take_along_axis(teacher_logits, clipped, axis=1), 0.0)
    draft_local = jnp.where(inside, jnp.take_along_axis(draft_logits, clipped, axis=1), 0.0)
    local_max = jnp.max(draft_logits, axis=1)
    row_max = lax.pmax(local_max, ("dp", "section", "mp"))
    local_total = jnp.sum(jnp.exp(draft_logits - row_max[:, None]), axis=1)
    exp_total, teacher_pick, draft_pick = lax.psum(
        (local_total, teacher_local, draft_local), ("dp", "section", "mp")
    )
    log_total = row_max + jnp.log(exp_total)
    teach_log = jax.nn.log_softmax(teacher_pick, axis=1)
    teach_prob = jnp.exp(teach_log)
    token_loss = jnp.sum(teach_prob * (teach_log - draft_pick + log_total[:, None]), axis=1)
    loss_rows = lax.dynamic_slice_in_dim(token_loss, lax.axis_index("dp") * rows_dp, rows_dp, 0)
    draft_prob = jnp.exp(draft_logits - log_total[:, None])
    row_ids = jnp.broadcast_to(
        jnp.arange(total_rows, dtype=jnp.int32)[:, None], teacher_index.shape
    )
    placed = jnp.where(inside, teach_prob, 0.0)
    logit_grad = draft_prob.at[row_ids, clipped].add(-placed).astype(jnp.bfloat16)
    token_part = lax.psum_scatter(
        jnp.dot(logit_grad, head, preferred_element_type=jnp.float32),
        ("section", "mp"),
        scatter_dimension=0,
        tiled=True,
    )
    hidden_grad = lax.psum_scatter(token_part, "dp", scatter_dimension=1, tiled=True)
    weighted = hidden_grad * draft_gain[None, :]
    inner = lax.psum(jnp.sum(weighted * joined, axis=1), "dp")
    joined_grad = (
        draft_scale[:, None] * weighted - joined * (draft_scale**3 * inner / D)[:, None]
    ).astype(jnp.bfloat16)
    gain_grad = lax.psum(
        jnp.sum(hidden_grad * joined * draft_scale[:, None], axis=0), ("section", "mp")
    )
    tok_rows = gathered
    weight_grad = jnp.einsum(
        "jtf,tc->jfc",
        tok_rows,
        lax.all_gather(joined_grad, ("section", "mp"), axis=0, tiled=True),
        preferred_element_type=jnp.float32,
    )
    return (weight_grad.astype(jnp.bfloat16), gain_grad, loss_rows)


def solution(mesh):
    return jax.shard_map(
        shards,
        mesh=mesh,
        in_specs=(
            P(None, "dp", ("section", "mp")),
            P(None, ("section", "mp"), "dp"),
            P(("dp", "section", "mp"), None),
            P("dp"),
            P(("section", "mp")),
            P(),
        ),
        out_specs=(P(None, ("section", "mp"), "dp"), P("dp"), P("dp")),
        check_vma=False,
    )
```

profile of v0, /device:TPU:1, one launch (start us, length us, event | category | flops | bytes accessed | tf_op | source)
XLA Modules:
  0.0 1297.0 jit_solution(11186038379029137752)
XLA Ops:
  7.3 23.6 %all_gather.15 = bf16[3,128,256]{2,1,0:T(8,128)(2,1)S(1)} all-gather(bf16[3,16,256]{2,1,0:T(8,128)(2,1)} %param.8), channel_id=1, replica_groups=mesh['dp'=8,'section'=2,'mp'=16] {'dp'}, dimensions={1}, use_global_device_ids=true | all-gather | bytes 221184 | tf_op jit(solution)/shard_map/all_gather | solution.py:14
  30.9 1.2 convolution_bitcast_fusion
  32.2 79.9 %psum.51 = f32[128]{0:T(128)S(1)} all-reduce(f32[128]{0:T(128)S(1)} %fusion.2), channel_id=1, replica_groups=mesh['dp'=8,'section'=2,'mp'=16] {'section','mp'}, use_global_device_ids=true, to_apply=%region_8.9 | all-reduce | flops 128 | bytes 1024 | tf_op jit(solution)/shard_map/psum | solution.py:28
  114.1 221.6 %all-reduce.6.cloned.1.call-done = f32[128,1024]{1,0:T(8,128)} async-done(((f32[128,1024]{1,0:T(8,128)}), f32[128,1024]{1,0:T(8,128)}) %all-reduce.6.cloned.1.call-update) | async-done | bytes 524304
  335.7 0.9 multiply_reduce_fusion.4
  336.6 14.9 %psum.49 = f32[4]{0:T(128)S(1)} all-reduce(f32[4]{0:T(128)S(1)} %multiply_reduce_fusion.4), channel_id=1, replica_groups=mesh['dp'=8,'section'=2,'mp'=16] {'dp'}, use_global_device_ids=true, to_apply=%region_2.0 | all-reduce | flops 4 | bytes 32 | tf_op jit(solution)/shard_map/psum | solution.py:24
  351.5 0.8 multiply_convert_fusion
  352.4 23.9 %all_gather.16 = bf16[4,8192]{1,0:T(4,128)(2,1)} all-gather(bf16[4,1024]{1,0:T(4,128)(2,1)S(1)} %multiply_convert_fusion), channel_id=1, replica_groups=mesh['dp'=8,'section'=2,'mp'=16] {'dp'}, dimensions={1}, use_global_device_ids=true | all-gather | bytes 73728 | tf_op jit(solution)/shard_map/all_gather | solution.py:38
  377.0 37.8 %all-gather.5.cloned.1.call-done = bf16[128,8192]{1,0:T(8,128)(2,1)} async-done(((bf16[128,256]{1,0:T(8,128)(2,1)}), bf16[128,8192]{1,0:T(8,128)(2,1)}) %all-gather.5.cloned.1.call-update) | async-done | bytes 2097168 | tf_op jit(solution)/shard_map/all_gather | solution.py:33
  414.8 5.6 fusion.13
  420.4 26.5 %gather_fusion = f32[4096]{0:T(1024)S(1)} fusion(f32[128,501]{0,1:T(8,128)S(1)} %fusion.13, s32[4096]{0:T(1024)S(1)} %reshape.80), kind=kCustom, calls=%fused_computation.clone | custom fusion | bytes 65536 | tf_op jit(solution)/shard_map/jit(take_along_axis)/gather | solution.py:49
  447.0 47.2 %all-gather.7.cloned.1.call-done = bf16[32,4,8192]{2,1,0:T(4,128)(2,1)} async-done(((bf16[1,4,8192]{2,1,0:T(4,128)(2,1)}), bf16[32,4,8192]{2,1,0:T(4,128)(2,1)}) %all-gather.7.cloned.1.call-update) | async-done | bytes 2097168 | tf_op jit(solution)/shard_map/all_gather | solution.py:40
  494.2 4.0 reshape.76
  498.1 5.6 fusion.12
  503.7 74.7 %pmax.7 = f32[128]{0:T(128)S(1)} all-reduce(f32[128]{0:T(128)S(1)} %get-tuple-element.29), channel_id=1, replica_groups=mesh['dp'=8,'section'=2,'mp'=16] {'dp','section','mp'}, use_global_device_ids=true, to_apply=%region_4.0 | all-reduce | flops 128 | bytes 1024 | tf_op jit(solution)/shard_map/pmax | solution.py:52
  578.4 26.5 %gather_fusion.1 = f32[4096]{0:T(1024)S(1)} fusion(f32[128,501]{0,1:T(8,128)S(1)} %get-tuple-element.30, s32[4096]{0:T(1024)S(1)} %reshape.80), kind=kCustom, calls=%fused_computation.1.clone | custom fusion | bytes 65536 | tf_op jit(solution)/shard_map/jit(take_along_axis)/gather | solution.py:50
  605.2 74.3 %all-reduce.2 = (f32[128]{0:T(128)S(1)}, f32[128,32]{1,0:T(8,128)S(1)}, f32[128,32]{1,0:T(8,128)S(1)}) all-reduce(f32[128]{0:T(128)S(1)} %exponential_reduce_fusion, f32[128,32]{1,0:T(8,128)S(1)} %select_select_fusion.1, f32[128,32]{1,0:T(8,128)S(1)} %get-tuple-element.24), channel_id=1, replica_groups=mesh['dp'=8,'section'=2,'mp'=16] {'dp','section','mp'}, use_global_device_ids=true, to_apply=%region_6.7 | all-reduce | flops 8320 | bytes 66560 | tf_op jit(solution)/shard_map/psum | solution.py:54
  680.2 27.9 %scatter_fusion = f32[64128]{0:T(1024)S(1)} fusion(f32[64128]{0:T(1024)S(1)} %exponential_bitcast_fusion, s32[4096]{0:T(1024)S(1)} %reshape.59, f32[4096]{0:T(1024)S(1)} %reshape.61), kind=kCustom, calls=%fused_computation.2 | custom fusion | flops 4096 | bytes 65536
  708.1 7.0 fusion.5
  715.2 310.0 %all-reduce.8.cloned.1.call-done = f32[128,8192]{1,0:T(8,128)} async-done(((f32[128,8192]{1,0:T(8,128)}), f32[128,8192]{1,0:T(8,128)}) %all-reduce.8.cloned.1.call-update) | async-done | bytes 4194320
  1025.2 1.0 constant_dynamic-slice_fusion
  1026.2 2.6 copy.29
  1029.4 90.1 %reduce-scatter.4.cloned.1.call-done = f32[1024,4]{1,0:T(8,128)} async-done(((f32[8192,4]{1,0:T(8,128)}), f32[1024,4]{1,0:T(8,128)}) %reduce-scatter.4.cloned.1.call-update) | async-done | bytes 16400
  1119.6 1.2 copy.30
  1120.8 1.0 multiply_reduce_fusion.2
  1121.7 71.9 %psum.54 = f32[1024]{0:T(1024)} all-reduce(f32[1024]{0:T(1024)S(1)} %get-tuple-element.19), channel_id=1, replica_groups=mesh['dp'=8,'section'=2,'mp'=16] {'section','mp'}, use_global_device_ids=true, to_apply=%region_18.20 | all-reduce | flops 1024 | bytes 8192 | tf_op jit(solution)/shard_map/psum | solution.py:80
  1193.7 14.5 %psum.53 = f32[4]{0:T(128)S(1)} all-reduce(f32[4]{0:T(128)S(1)} %get-tuple-element.20), channel_id=1, replica_groups=mesh['dp'=8,'section'=2,'mp'=16] {'dp'}, use_global_device_ids=true, to_apply=%region_16.18 | all-reduce | flops 4 | bytes 32 | tf_op jit(solution)/shard_map/psum | solution.py:76
  1208.2 0.8 fusion.9
  1209.0 77.3 %all-gather.1 = bf16[32,4,1024]{2,1,0:T(4,128)(2,1)S(1)} all-gather(bf16[1,4,1024]{2,1,0:T(4,128)(2,1)S(1)} %fusion.9), channel_id=1, replica_groups=mesh['dp'=8,'section'=2,'mp'=16] {'section','mp'}, dimensions={0}, use_global_device_ids=true | all-gather | bytes 270336 | tf_op jit(solution)/shard_map/all_gather | solution.py:87
  1286.4 0.8 reshape.78
  1287.1 1.5 fusion
  1288.7 1.7 copy.26
  (54 shorter events, 3.9 us)
Async XLA Ops:
  7.2 23.7 %copy-start = (bf16[3,256,1024]{2,1,0:T(8,128)(2,1)S(1)}, bf16[3,256,1024]{2,1,0:T(8,128)(2,1)}, u32[]{:S(2)}) copy-start(bf16[3,256,1024]{2,1,0:T(8,128)(2,1)} %param.9) | copy-start | bytes 4718596
  7.2 105.7 %copy-start.6 = (u32[256]{0:T(256)S(1)}, u32[256]{0:T(256)}, u32[]{:S(2)}) copy-start(u32[256]{0:T(256)} %constant.109) | copy-start | bytes 3076
  7.2 369.5 %copy-start.5 = (s32[2]{0:T(128)S(1)}, s32[2]{0:T(128)}, u32[]{:S(2)}) copy-start(s32[2]{0:T(128)} %constant.61) | copy-start | bytes 28
  7.2 369.5 %copy-start.4 = (s32[2]{0:T(128)S(1)}, s32[2]{0:T(128)}, u32[]{:S(2)}) copy-start(s32[2]{0:T(128)} %constant.64) | copy-start | bytes 28
  7.2 104.9 %copy-start.3 = (f32[256]{0:T(256)S(1)}, f32[256]{0:T(256)}, u32[]{:S(2)}) copy-start(f32[256]{0:T(256)} %param.12) | copy-start | bytes 3076
  7.2 344.3 %copy-start.1 = (f32[1024]{0:T(1024)S(1)}, f32[1024]{0:T(1024)}, u32[]{:S(2)}) copy-start(f32[1024]{0:T(1024)} %param.11) | copy-start | bytes 12292
  7.2 369.1 %copy-start.2 = (s32[128,32]{0,1:T(8,128)S(1)}, s32[128,32]{0,1:T(8,128)}, u32[]{:S(2)}) copy-start(s32[128,32]{0,1:T(8,128)} %param.13) | copy-start | bytes 49156
  7.2 328.5 %all-reduce.6.cloned.1.call-start = ((), (), s32[]{:S(2)}) async-start(), calls=%async_computation.4 | async-start | bytes 1048576
  32.1 382.7 %all-gather.5.cloned.1.call-start = ((), (), s32[]{:S(2)}) async-start(), calls=%async_computation.1 | async-start | bytes 2162688 | tf_op jit(solution)/shard_map/all_gather | solution.py:33
  112.8 381.3 %all-gather.7.cloned.1.call-start = ((), (), s32[]{:S(2)}) async-start(), calls=%async_computation.2 | async-start | bytes 2162688 | tf_op jit(solution)/shard_map/all_gather | solution.py:40
  376.3 648.9 %all-reduce.8.cloned.1.call-start = ((), (), s32[]{:S(2)}) async-start(), calls=%async_computation.5 | async-start | bytes 8388608
  715.2 404.4 %reduce-scatter.4.cloned.1.call-start = ((), (), s32[]{:S(2)}) async-start(), calls=%async_computation.3 | async-start | bytes 4718592
Sparse Core Ops, SparseCore 0:
  32.2 303.5 all-reduce.5
  338.6 76.1 all-gather.4
  418.0 76.1 all-gather.6
  715.3 309.8 all-reduce.7
  1028.9 90.5 reduce-scatter.3
where the time goes:
time: 1300 us
  waiting for transfers between devices  707 us (54%)
  blocking collectives  455 us (35%)
  local copies, waits for them, and re-layouts  66.2 us (5%)
  other arithmetic  33.2 us (3%)
  matrix products  20.9 us (2%)
  between operations  14.7 us (1%)
    unnamed x8, waiting for transfers between devices  622 us
    psum x1, blocking collectives, shards(): lax.psum(jnp.sum(high_state * high_state, axis=1), ('section', 'mp'))  79.9 us
    all_gather x1, blocking collectives, shards(): lax.all_gather(joined_grad, ('section', 'mp'), axis=0, tiled=True)  77.3 us
    pmax x1, blocking collectives, shards(): row_max = lax.pmax(local_max, ('dp', 'section', 'mp'))  74.7 us
    psum x1, blocking collectives, shards(): lax.psum((local_total, teacher_local, draft_local), ('dp', 'section', 'mp'))  74.3 us
    psum x1, blocking collectives, shards(): lax.psum(jnp.sum(hidden_grad * joined * draft_scale[:, None], axis=0), ('...  71.9 us
    all_gather x1, waiting for transfers between devices, shards(): lax.all_gather(wide_rows, ('section', 'mp'), axis=0, tiled=True)  47.2 us
    all_gather x1, waiting for transfers between devices, shards(): lax.all_gather(teacher_in, ('section', 'mp'), axis=1, tiled=True)  37.8 us
  transfers between devices with their start and end apart: 5, of which 5 were waited for; matrix products, arithmetic and copies ran while one was open for 3% of the time, Pallas kernels for 0%

commit v1 on v0

v1 whole, which is shorter than its diff:
```python
import jax
import jax.numpy as jnp
from jax import lax
from jax.experimental import pallas as pl
from jax.experimental.pallas import tpu as pltpu
from jax.sharding import PartitionSpec as P

D = 8192
EPS = 1e-05
VOC = 501
ROWS = 512
LOW = -1e30
F32 = jnp.float32
BF16 = jnp.bfloat16
MESH = pl.DeviceIdType.MESH

(A1, T1, TG, B0, TSQ, B1, T2, T3, S0, S1, C1, U1, U2, U3, V1, V2, V3, R1, R2, I0, I1, GM, JM, GS, JS) = range(25)
STAGES = 25


def kernel(
    feat, fc_hbm, head_hbm, dgain, tgain, index,
    feat_out, grad_out, gain_out, loss_out,
    head, fc, featg, part, brecv0, bsum, brecv1, traw, tgain_s, tgain_r, tsq_s, tsq_r, xt, xd, joined,
    sq_s, sq_r0, sq_s1, sq_r1, mask, lt, ld, placed, grad,
    us1, ur1, us2, ur2, us3, ur3, vs1, vr1, vs2, vr2, vs3, vr3,
    hf, hb, r0, r1s, r1r, r2s, r2r, in_s, in_r0, in_s1, in_r1, gp_s, gp_r, gs_s, gs_r, jg,
    load_sem, ssem, rsem, c2s, c2r, c3s, c3r, r0s, r0r,
):
    d = lax.axis_index("dp")
    c = lax.axis_index("section")
    m = lax.axis_index("mp")
    z = m // 2
    yh = m % 2
    p = d * 2 + yh
    sib = (d, 1 - c, m)

    load_fc = pltpu.make_async_copy(fc_hbm, fc, load_sem.at[0])
    load_head = pltpu.make_async_copy(head_hbm, head, load_sem.at[1])
    load_fc.start()
    load_head.start()

    barrier = pltpu.get_barrier_semaphore()
    pl.semaphore_signal(barrier, inc=1, device_id=sib, device_id_type=MESH)

    @pl.loop(1, 16)
    def _(i):
        pl.semaphore_signal(barrier, inc=1, device_id=(d, c, (m + i) % 16), device_id_type=MESH)

    @pl.loop(2, 16)
    def _(i):
        pl.semaphore_signal(
            barrier, inc=1, device_id=((d + i // 2) % 8, c, z * 2 + i % 2), device_id_type=MESH
        )

    pl.semaphore_wait(barrier, 30)

    def send(src, dst, stage, dev):
        pltpu.make_async_remote_copy(
            src_ref=src, dst_ref=dst, send_sem=ssem.at[stage], recv_sem=rsem.at[stage],
            device_id=dev, device_id_type=MESH,
        ).start()

    def arrived(ref, stage):
        pltpu.make_async_copy(ref, ref, rsem.at[stage]).wait()

    def sent(ref, stage):
        pltpu.make_async_copy(ref, ref, ssem.at[stage]).wait()

    def to_mp(src, dst, stage):
        @pl.loop(1, 16)
        def _(i):
            send(src, dst, stage, (d, c, (m + i) % 16))

    def to_dp(src, dst, stage):
        @pl.loop(1, 8)
        def _(i):
            send(src, dst, stage, ((d + i) % 8, c, m))

    def to_z(src, dst, stage):
        @pl.loop(1, 8)
        def _(i):
            send(src, dst, stage, (d, c, ((z + i) % 8) * 2 + yh))

    def to_plane(src, dst, stage):
        @pl.loop(1, 16)
        def _(i):
            q = (p + i) % 16
            send(src, dst, stage, (q // 2, c, z * 2 + q % 2))

    to_dp(feat, featg.at[d], A1)
    to_mp(feat.at[2], traw.at[m], T1)
    tgain_s[...] = jnp.broadcast_to(tgain[...], (8, 256))
    to_mp(tgain_s, tgain_r.at[m], TG)
    featg[d] = feat[...]
    traw[m] = feat[2]
    tgain_r[m] = tgain_s[...]

    start = ((d * 2 + c) * 16 + m) * VOC
    local = jnp.transpose(index[...]) - start

    @pl.loop(0, ROWS // 64)
    def _(i):
        rows = lax.broadcasted_iota(jnp.int32, (64, 128), 0) + i * 64
        hit = rows == local[0:1, :]
        for k in range(1, 32):
            hit = hit | (rows == local[k : k + 1, :])
        hit = hit & (rows < VOC)
        mask[pl.ds(pl.multiple_of(i * 64, 64), 64), :] = hit.astype(F32)

    load_fc.wait()
    arrived(featg.at[pl.ds(0, 7)], A1)
    for half in range(4):
        cols = slice(half * 256, half * 256 + 256)
        acc = jnp.dot(featg[:, 0].reshape(128, 256), fc[0, :, cols], preferred_element_type=F32)
        for j in (1, 2):
            acc += jnp.dot(featg[:, j].reshape(128, 256), fc[j, :, cols], preferred_element_type=F32)
        for zz in range(8):
            part[half // 2, zz * 2 + half % 2] = acc[zz * 16 : zz * 16 + 16]
    send(part.at[1 - c], brecv0, B0, sib)

    arrived(traw.at[pl.ds(0, 15)], T1)
    arrived(tgain_r.at[pl.ds(0, 15)], TG)
    tsq = jnp.zeros((16, 256), F32)
    for k in range(16):
        row = traw[k].astype(F32)
        tsq += row * row
    tsq = tsq[:, :128] + tsq[:, 128:]
    tsq_s[...] = tsq
    send(tsq_s, tsq_r, TSQ, sib)

    arrived(brecv0, B0)
    bsum[...] = part[c] + brecv0[...]

    @pl.loop(1, 16)
    def _(i):
        k = (m + i) % 16
        send(bsum.at[k], brecv1.at[m], B1, (d, c, k))

    brecv1[m] = bsum[m]

    arrived(tsq_r, TSQ)
    tsum = jnp.sum(tsq_s[...] + tsq_r[...], axis=1, keepdims=True)
    tscale = lax.rsqrt(tsum / D + EPS)
    for k in range(16):
        xt[c, d, k] = (traw[k].astype(F32) * tscale * tgain_r[k][0:1, :]).astype(BF16)
    to_dp(xt.at[c, d], xt.at[c, d], T2)

    arrived(brecv1.at[pl.ds(0, 15)], B1)
    js = brecv1[0]
    for k in range(1, 16):
        js += brecv1[k]
    joined[...] = js

    sq = js * js
    sq_s[...] = sq[:, :128] + sq[:, 128:]
    send(sq_s, sq_r0, S0, sib)
    arrived(sq_r0, S0)
    sq_s1[...] = sq_s[...] + sq_r0[...]
    to_plane(sq_s1, sq_r1.at[p], S1)
    sq_r1[p] = sq_s1[...]
    arrived(sq_r1.at[pl.ds(0, 15)], S1)
    total = sq_r1[0]
    for k in range(1, 16):
        total += sq_r1[k]
    dscale = lax.rsqrt(jnp.sum(total, axis=1, keepdims=True) / D + EPS)
    own_cols = pl.multiple_of((c * 2 + yh) * 256, 256)
    gain = dgain[:, pl.ds(own_cols, 256)]
    xd[c, p, z] = (js * dscale * gain).astype(BF16)
    to_z(xd.at[c, p, z], xd.at[c, p, z], C1)

    arrived(xt.at[c, pl.ds(0, 7)], T2)
    send(xt.at[c], xt.at[c], T3, sib)

    arrived(xd.at[c, p, pl.ds(0, 7)], C1)

    def c2(i):
        q = (p + i) % 16
        return pltpu.make_async_remote_copy(
            src_ref=xd.at[c, p], dst_ref=xd.at[c, p], send_sem=c2s, recv_sem=c2r.at[p],
            device_id=(q // 2, c, z * 2 + q % 2), device_id_type=MESH,
        )

    def c3(q):
        return pltpu.make_async_remote_copy(
            src_ref=xd.at[c, q], dst_ref=xd.at[c, q], send_sem=c3s, recv_sem=c3r,
            device_id=sib, device_id_type=MESH,
        )

    @pl.loop(1, 16)
    def _(i):
        c2(i).start()

    c3(p).start()

    load_head.wait()
    arrived(xt.at[1 - c], T3)
    lt[...] = jnp.zeros_like(lt)

    @pl.loop(0, 8)
    def _(i):
        cc = i // 4
        mm = (i % 4) * 4
        x = jnp.concatenate([xt[cc, :, mm + k].reshape(128, 256) for k in range(4)], axis=1)
        cols = pl.ds(pl.multiple_of(i * 1024, 1024), 1024)
        lt[...] += lax.dot_general(head[:, cols], x, (((1,), (1,)), ((), ())), preferred_element_type=F32)

    on = mask[0:VOC, :] > 0.5
    logits = jnp.where(on, lt[...], LOW)
    tmax = jnp.max(logits, axis=0, keepdims=True)
    away = logits - tmax
    e = jnp.where(on, jnp.exp(away), 0.0)
    tz = jnp.sum(e, axis=0, keepdims=True)
    tw = jnp.sum(jnp.where(on, e * away, 0.0), axis=0, keepdims=True)

    def rows_of(a, b, w):
        return jnp.concatenate([a, b, w, jnp.zeros((5, 128), F32)], axis=0)

    def merge_t(ref):
        a = ref[...]
        top = jnp.max(a[:, 0:1, :], axis=0)
        low = a[:, 0:1, :] - top[None]
        f = jnp.exp(low)
        zz = jnp.sum(f * a[:, 1:2, :], axis=0)
        ww = jnp.sum(f * (a[:, 2:3, :] + jnp.where(a[:, 1:2, :] > 0.0, low, 0.0) * a[:, 1:2, :]), axis=0)
        return top, zz, ww

    def merge_d(ref):
        a = ref[...]
        top = jnp.max(a[:, 0:1, :], axis=0)
        f = jnp.exp(a[:, 0:1, :] - top[None])
        return top, jnp.sum(f * a[:, 1:2, :], axis=0), jnp.sum(a[:, 2:3, :], axis=0)

    us1[...] = rows_of(tmax, tz, tw)
    to_z(us1, ur1.at[z], U1)
    ur1[z] = us1[...]

    @pl.loop(1, 16)
    def _(i):
        q = (p + 16 - i) % 16
        pltpu.make_async_copy(xd.at[c, q], xd.at[c, q], c2r.at[q]).wait()
        c3(q).start()

    arrived(ur1.at[pl.ds(0, 7)], U1)
    us2[...] = rows_of(*merge_t(ur1))
    to_plane(us2, ur2.at[p], U2)
    ur2[p] = us2[...]
    arrived(ur2.at[pl.ds(0, 15)], U2)
    us3[...] = rows_of(*merge_t(ur2))
    send(us3, ur3.at[c], U3, sib)
    ur3[c] = us3[...]

    pltpu.make_async_copy(xd.at[1 - c], xd.at[1 - c], c3r).wait()
    ld[...] = jnp.zeros_like(ld)

    @pl.loop(0, 8)
    def _(i):
        x = jnp.concatenate([xd[k // 2, i * 2 + k % 2].reshape(128, 256) for k in range(4)], axis=1)
        cols = pl.ds(pl.multiple_of(i * 1024, 1024), 1024)
        ld[...] += lax.dot_general(head[:, cols], x, (((1,), (1,)), ((), ())), preferred_element_type=F32)

    arrived(ur3.at[1 - c], U3)
    tmax, tz, tw = merge_t(ur3)
    tp = jnp.where(mask[0:VOC, :] > 0.5, jnp.exp(jnp.minimum(lt[...] - tmax, 0.0)) / tz, 0.0)
    placed[...] = tp
    teach = tw / tz - jnp.log(tz)

    logits = ld[...]
    dmax = jnp.max(logits, axis=0, keepdims=True)
    dz = jnp.sum(jnp.exp(logits - dmax), axis=0, keepdims=True)
    dw = jnp.sum(tp * logits, axis=0, keepdims=True)
    vs1[...] = rows_of(dmax, dz, dw)
    to_z(vs1, vr1.at[z], V1)
    vr1[z] = vs1[...]
    arrived(vr1.at[pl.ds(0, 7)], V1)
    vs2[...] = rows_of(*merge_d(vr1))
    to_plane(vs2, vr2.at[p], V2)
    vr2[p] = vs2[...]
    arrived(vr2.at[pl.ds(0, 15)], V2)
    vs3[...] = rows_of(*merge_d(vr2))
    send(vs3, vr3.at[c], V3, sib)
    vr3[c] = vs3[...]
    arrived(vr3.at[1 - c], V3)
    dmax, dz, dw = merge_d(vr3)
    log_total = dmax + jnp.log(dz)
    loss = teach - dw + log_total
    loss_out[...] = pltpu.roll(jnp.broadcast_to(loss, (8, 128)), (128 - d * 16) % 128, 1)

    g = jnp.exp(ld[...] - log_total) - placed[...]
    grad[...] = jnp.zeros_like(grad)
    grad[0:VOC, :] = g
    grad_rows = jnp.transpose(grad[...])[:, 0:VOC].astype(BF16)

    def r0_copy(dd):
        return pltpu.make_async_remote_copy(
            src_ref=hb.at[1 - c, pl.ds(dd * 2, 2)], dst_ref=r0.at[pl.ds(dd * 2, 2)],
            send_sem=r0s, recv_sem=r0r.at[dd], device_id=sib, device_id_type=MESH,
        )

    def compute(dd):
        for k in range(4):
            cols = pl.ds(pl.multiple_of(dd * 1024 + k * 256, 256), 256)
            h = jnp.dot(grad_rows, head[:, cols], preferred_element_type=F32)
            hf[k // 2, dd * 2 + k % 2] = h
            hb[k // 2, dd * 2 + k % 2] = h.astype(BF16)
        r0_copy(dd).start()

    def add_up(dd):
        pltpu.make_async_copy(r0.at[pl.ds(dd * 2, 2)], r0.at[pl.ds(dd * 2, 2)], r0r.at[dd]).wait()
        for k in range(2):
            q = dd * 2 + k
            r1s[q] = (hf[c, q] + r0[q].astype(F32)).astype(BF16)

    def to_peer(q):
        send(r1s.at[q], r1r.at[p], R1, (q // 2, c, z * 2 + q % 2))

    compute((d + 1) % 8)

    @pl.loop(2, 9)
    def _(i):
        compute((d + i) % 8)
        dd = (d + i - 1) % 8
        add_up(dd)
        to_peer(dd * 2)
        to_peer(dd * 2 + 1)

    add_up(d)
    to_peer(d * 2 + 1 - yh)
    r1r[p] = r1s[p]
    arrived(r1r.at[pl.ds(0, 15)], R1)
    for zz in range(8):
        acc = r1r[0, zz * 16 : zz * 16 + 16].astype(F32)
        for k in range(1, 16):
            acc += r1r[k, zz * 16 : zz * 16 + 16].astype(F32)
        r2s[zz] = acc.astype(BF16)

    @pl.loop(1, 8)
    def _(i):
        zz = (z + i) % 8
        send(r2s.at[zz], r2r.at[z], R2, (d, c, zz * 2 + yh))

    r2r[z] = r2s[z]
    arrived(r2r.at[pl.ds(0, 7)], R2)
    hidden = r2r[0].astype(F32)
    for k in range(1, 8):
        hidden += r2r[k].astype(F32)

    js = joined[...]
    weighted = hidden * gain
    inner = weighted * js
    in_s[...] = inner[:, :128] + inner[:, 128:]
    send(in_s, in_r0, I0, sib)
    gp = hidden * js * dscale
    gp_s[...] = gp[0:8] + gp[8:16]
    to_mp(gp_s, gp_r.at[m], GM)
    gp_r[m] = gp_s[...]
    arrived(in_r0, I0)
    in_s1[...] = in_s[...] + in_r0[...]
    to_plane(in_s1, in_r1.at[p], I1)
    in_r1[p] = in_s1[...]
    arrived(gp_r.at[pl.ds(0, 15)], GM)
    for k in range(2):
        acc = gp_r[k]
        for zz in range(1, 8):
            acc += gp_r[zz * 2 + k]
        gs_s[k] = acc
    send(gs_s, gs_r.at[c], GS, sib)
    gs_r[c] = gs_s[...]
    arrived(in_r1.at[pl.ds(0, 15)], I1)
    total = in_r1[0]
    for k in range(1, 16):
        total += in_r1[k]
    inner = jnp.sum(total, axis=1, keepdims=True)
    jg[c, m] = (dscale * weighted - js * (dscale * dscale * dscale * inner / D)).astype(BF16)
    to_mp(jg.at[c, m], jg.at[c, m], JM)
    feat_out[...] = jnp.concatenate(
        [jnp.concatenate([featg[k, j : j + 1] for k in range(8)], axis=1) for j in range(3)], axis=0
    )
    arrived(gs_r.at[1 - c], GS)
    for k in range(4):
        gain_out[:, k * 256 : k * 256 + 256] = jnp.sum(gs_r[k // 2, k % 2], axis=0, keepdims=True)
    arrived(jg.at[c, pl.ds(0, 15)], JM)
    send(jg.at[c], jg.at[c], JS, sib)
    arrived(jg.at[1 - c], JS)
    for k in range(4):
        for zz in range(8):
            grad_out[zz * 16 : zz * 16 + 16, k * 256 : k * 256 + 256] = jg[k // 2, zz * 2 + k % 2]

    sent(featg.at[pl.ds(0, 7)], A1)
    sent(traw.at[pl.ds(0, 15)], T1)
    sent(tgain_r.at[pl.ds(0, 15)], TG)
    sent(brecv0, B0)
    sent(tsq_s, TSQ)
    sent(bsum.at[pl.ds(0, 15)], B1)
    sent(xt.at[c, pl.ds(0, 7)], T2)
    sent(xt.at[c], T3)
    sent(sq_s, S0)
    sent(sq_r1.at[pl.ds(0, 15)], S1)
    sent(xd.at[c, p, pl.ds(0, 7)], C1)
    pltpu.make_async_copy(xd.at[c, pl.ds(0, 15)], xd.at[c, pl.ds(0, 15)], c2s).wait()
    pltpu.make_async_copy(xd.at[c], xd.at[c], c3s).wait()
    sent(ur1.at[pl.ds(0, 7)], U1)
    sent(ur2.at[pl.ds(0, 15)], U2)
    sent(us3, U3)
    sent(vr1.at[pl.ds(0, 7)], V1)
    sent(vr2.at[pl.ds(0, 15)], V2)
    sent(vs3, V3)
    pltpu.make_async_copy(r0, r0, r0s).wait()
    sent(r1r.at[pl.ds(0, 15)], R1)
    sent(r2r.at[pl.ds(0, 7)], R2)
    sent(in_s, I0)
    sent(in_r1.at[pl.ds(0, 15)], I1)
    sent(gp_r.at[pl.ds(0, 15)], GM)
    sent(gs_s, GS)
    sent(jg.at[c, pl.ds(0, 15)], JM)
    sent(jg.at[c], JS)


def shards(features, fc_weight, head, draft_gain, target_gain, teacher_index):
    vmem = pl.BlockSpec(memory_space=pltpu.VMEM)
    hbm = pl.BlockSpec(memory_space=pl.ANY)
    V = pltpu.VMEM
    tile = V((16, 128), F32)
    tiles = V((16, 16, 128), F32)
    stat = [V((8, 128), F32), V((8, 8, 128), F32), V((8, 128), F32), V((16, 8, 128), F32), V((8, 128), F32), V((2, 8, 128), F32)]
    feat_all, joined_grad, gain_grad, loss = pl.pallas_call(
        kernel,
        out_shape=(
            jax.ShapeDtypeStruct((3, 128, 256), BF16),
            jax.ShapeDtypeStruct((128, 1024), BF16),
            jax.ShapeDtypeStruct((1, 1024), F32),
            jax.ShapeDtypeStruct((8, 128), F32),
        ),
        in_specs=[vmem, hbm, hbm, vmem, vmem, vmem],
        out_specs=(vmem, vmem, vmem, vmem),
        scratch_shapes=[
            V((VOC, D), BF16),
            V((3, 256, 1024), BF16),
            V((8, 3, 16, 256), BF16),
            V((2, 16, 16, 256), F32),
            V((16, 16, 256), F32),
            V((16, 16, 256), F32),
            V((16, 16, 256), F32),
            V((16, 16, 256), BF16),
            V((8, 256), F32),
            V((16, 8, 256), F32),
            tile,
            tile,
            V((2, 8, 16, 16, 256), BF16),
            V((2, 16, 8, 16, 256), BF16),
            V((16, 256), F32),
            tile, tile, tile, tiles,
            V((ROWS, 128), F32),
            V((VOC, 128), F32),
            V((VOC, 128), F32),
            V((VOC, 128), F32),
            V((ROWS, 128), F32),
            *stat,
            *stat,
            V((2, 16, 128, 256), F32),
            V((2, 16, 128, 256), BF16),
            V((16, 128, 256), BF16),
            V((16, 128, 256), BF16),
            V((16, 128, 256), BF16),
            V((8, 16, 256), BF16),
            V((8, 16, 256), BF16),
            tile, tile, tile, tiles,
            V((8, 256), F32),
            V((16, 8, 256), F32),
            V((2, 8, 256), F32),
            V((2, 2, 8, 256), F32),
            V((2, 16, 16, 256), BF16),
            pltpu.SemaphoreType.DMA((2,)),
            pltpu.SemaphoreType.DMA((STAGES,)),
            pltpu.SemaphoreType.DMA((STAGES,)),
            pltpu.SemaphoreType.DMA,
            pltpu.SemaphoreType.DMA((16,)),
            pltpu.SemaphoreType.DMA,
            pltpu.SemaphoreType.DMA,
            pltpu.SemaphoreType.DMA,
            pltpu.SemaphoreType.DMA((8,)),
        ],
        compiler_params=pltpu.CompilerParams(
            collective_id=0, has_side_effects=True, vmem_limit_bytes=52 * 2**20
        ),
        cost_estimate=pl.CostEstimate(flops=3_600_000_000, bytes_accessed=12_000_000, transcendentals=200_000),
    )(features, fc_weight, head, draft_gain.reshape(1, 1024), target_gain.reshape(1, 256), teacher_index)
    weight_grad = jnp.einsum("jtf,tc->jfc", feat_all, joined_grad, preferred_element_type=F32)
    return (weight_grad.astype(BF16), gain_grad.reshape(1024), loss[0, :16])


def solution(mesh):
    return jax.shard_map(
        shards,
        mesh=mesh,
        in_specs=(
            P(None, "dp", ("section", "mp")),
            P(None, ("section", "mp"), "dp"),
            P(("dp", "section", "mp"), None),
            P("dp"),
            P(("section", "mp")),
            P(),
        ),
        out_specs=(P(None, ("section", "mp"), "dp"), P("dp"), P("dp")),
        check_vma=False,
    )
```

time: 1300 us -> 130 us (0.10)
  waiting for transfers between devices: 707 us -> 0 us
  blocking collectives: 455 us -> 0 us
  Pallas kernels: 0 us -> 123 us
  local copies, waits for them, and re-layouts: 66.2 us -> 4.02 us
  other arithmetic: 33.2 us -> 0 us
  matrix products: 20.9 us -> 1.74 us
  between operations: 14.7 us -> 0.65 us
    unnamed x8 -> x0, waiting for transfers between devices: 622 us -> none
    psum x5 -> x0, blocking collectives: 256 us -> none  [the longest x1 79.9 us: shards(): lax.psum(jnp.sum(high_state * high_state, axis=1), ('section', 'mp'))]
    all_gather x3 -> x0, blocking collectives: 125 us -> none  [the longest x1 77.3 us: shards(): lax.all_gather(joined_grad, ('section', 'mp'), axis=0, tiled=True)]
    pallas_call x0 -> x1, Pallas kernels: none -> 123 us  [shards(): pl.pallas_call(kernel, out_shape=(jax.ShapeDtypeStruct((3, 128, 256), BF1...]
    all_gather x2 -> x0, waiting for transfers between devices: 85 us -> none  [the longest x1 47.2 us: shards(): lax.all_gather(wide_rows, ('section', 'mp'), axis=0, tiled=True)]
    pmax x1 -> x0, blocking collectives: 74.7 us -> none  [shards(): row_max = lax.pmax(local_max, ('dp', 'section', 'mp'))]
    gather x5 -> x0, local copies, waits for them, and re-layouts: 53.3 us -> none  [the longest x3 26.7 us: shards(): jnp.take_along_axis(teacher_logits, clipped, axis=1)]
    unnamed x6 -> x0, other arithmetic: 29 us -> none
  transfers between devices with their start and end apart: 5 -> 0, of which waited for: 5 -> 0; matrix products, arithmetic and copies ran while one was open for 3% -> 0% of each run, Pallas kernels for 0% -> 0%
where the time goes in v1:
time: 130 us; the launch traced here: 129 us
  Pallas kernels  123 us (95%)
  local copies, waits for them, and re-layouts  4.02 us (3%)
  matrix products  1.74 us (1%)
    pallas_call x1, Pallas kernels, shards(): pl.pallas_call(kernel, out_shape=(jax.ShapeDtypeStruct((3, 128, 256), BF1...  123 us
    unnamed x8, local copies, waits for them, and re-layouts  3.51 us

profile of v1, /device:TPU:1, one launch (start us, length us, event | category | flops | bytes accessed | tf_op | source)
XLA Modules:
  0.0 129.4 jit_solution(13257910215247872290)
XLA Ops:
  0.6 0.8 copy.9.index
  1.4 0.0 copy-start
  1.5 0.7 copy-done
  2.2 0.0 copy-start.1
  2.2 0.7 copy-done.1
  2.9 0.0 copy-start.2
  2.9 0.7 copy-done.2
  3.6 123.0 %shard_map.85 = (bf16[3,128,256]{2,1,0:T(8,128)(2,1)S(1)}, bf16[128,1024]{1,0:T(8,128)(2,1)S(1)}, f32[1,1024]{1,0:T(1,128)S(1)}, f32[8,128]{1,0:T(8,128)S(1)}) custom-call(bf16[3,16,256]{2,1,0:T(8,128)(2,1)S(1)} %copy-done, bf16[3,256,1024]{2,1,0:T(8,128)(2,1)} %fc_hbm.1, bf16[501,8192]{1,0:T(8,128)(2,1)} %head_hbm.1, f32[1,1024]{1,0:T(1,128)S(1)} %bitcast.10, ...), custom_call_target="tpu_custom_call" | custom-call | flops 3600000000 | bytes 12000000 | tf_op jit(solution)/shard_map/pallas_call | solution.py:426
  126.6 0.5 slice_bitcast_fusion
  127.1 1.7 %convolution_convert_fusion = bf16[3,256,1024]{2,1,0:T(8,128)(2,1)} fusion(bf16[3,128,256]{2,1,0:T(8,128)(2,1)S(1)} %get-tuple-element.7, bf16[128,1024]{1,0:T(8,128)(2,1)S(1)} %get-tuple-element.8), kind=kOutput, calls=%fused_computation | convolution fusion | flops 202113024 | bytes 2031616 | tf_op jit(solution)/shard_map/jtf,tc->jfc/dot_general | solution.py:488
  128.8 0.6 copy.13
Async XLA Ops:
  1.4 0.7 copy-start
  2.2 0.7 copy-start.1
  2.9 0.7 copy-start.2

commit v2 on v1

v2 whole, which is shorter than its diff:
```python
import jax
import jax.numpy as jnp
from jax import lax
from jax.experimental import pallas as pl
from jax.experimental.pallas import tpu as pltpu
from jax.sharding import PartitionSpec as P

D = 8192
EPS = 1e-05
VOC = 501
ROWS = 512
LOW = -1e30
F32 = jnp.float32
BF16 = jnp.bfloat16
MESH = pl.DeviceIdType.MESH

(A1, T1, TG, TY, TX, T3, TGS, B0, B1, S1, C1, U1, U2, V1, V2, R1, R2, I1, GM, GS, JM, JS) = range(22)
STAGES = 22


def kernel(
    feat, fc_hbm, head_hbm, dgain_hbm, tgain_hbm, index_hbm,
    feat_out, grad_out, gain_out, loss_out,
    head, fc, featg, dgain, index, part, brecv0, bsum, brecv1, xr, tg, xd, joined,
    sq_s, sq_r, mask, lt, ld, placed, grad,
    us1, ur1, us2, ur2, vs1, vr1, vs2, vr2,
    hf, hb, r0, r1s, r1r, r2s, r2r, in_s, in_r, gp_s, gp_r, gs_s, gs_r, jg,
    load_sem, ssem, rsem, c2s, c2r, c3s, c3r, r0s, r0r,
):
    d = lax.axis_index("dp")
    c = lax.axis_index("section")
    m = lax.axis_index("mp")
    z = m // 2
    yh = m % 2
    p = d * 2 + yh
    sib = (d, 1 - c, m)

    loads = [
        pltpu.make_async_copy(src, dst, load_sem.at[k])
        for k, (src, dst) in enumerate((
            (feat, featg.at[d]), (feat.at[2], xr.at[c, d, m]), (tgain_hbm, tg.at[c, m]), (index_hbm, index),
            (dgain_hbm, dgain), (fc_hbm, fc), (head_hbm, head),
        ))
    ]
    for load in loads:
        load.start()
    load_feat, load_high, load_tg, load_index, load_dg, load_fc, load_head = loads

    barrier = pltpu.get_barrier_semaphore()

    @pl.loop(1, 16)
    def _(i):
        pl.semaphore_signal(barrier, inc=1, device_id=(d, c, (m + i) % 16), device_id_type=MESH)

    @pl.loop(1, 32)
    def _(i):
        k = (p * 2 + c + i) % 32
        pl.semaphore_signal(
            barrier, inc=1, device_id=(k // 4, k % 2, z * 2 + k // 2 % 2), device_id_type=MESH
        )

    pl.semaphore_wait(barrier, 46)

    def send(src, dst, stage, dev):
        pltpu.make_async_remote_copy(
            src_ref=src, dst_ref=dst, send_sem=ssem.at[stage], recv_sem=rsem.at[stage],
            device_id=dev, device_id_type=MESH,
        ).start()

    volume = {
        A1: featg.at[pl.ds(0, 7)], T1: xr.at[c, d, pl.ds(0, 15)], TG: tg.at[c, pl.ds(0, 15)], TY: xr.at[c, d],
        TX: xr.at[c, pl.ds(0, 6)], T3: xr.at[c], TGS: tg.at[c], B0: brecv0, B1: bsum.at[pl.ds(0, 15)],
        S1: sq_r.at[pl.ds(0, 31)], C1: xd.at[c, p, pl.ds(0, 7)], U1: ur1.at[pl.ds(0, 15)], U2: ur2.at[pl.ds(0, 15)],
        V1: vr1.at[pl.ds(0, 15)], V2: vr2.at[pl.ds(0, 15)], R1: r1r.at[pl.ds(0, 15)], R2: r2r.at[pl.ds(0, 7)],
        I1: in_r.at[pl.ds(0, 31)], GM: gp_r.at[pl.ds(0, 15)], GS: gs_s, JM: jg.at[c, pl.ds(0, 15)], JS: jg.at[c],
    }

    def arrived(stage):
        pltpu.make_async_copy(volume[stage], volume[stage], rsem.at[stage]).wait()

    def sent(stage):
        pltpu.make_async_copy(volume[stage], volume[stage], ssem.at[stage]).wait()

    def to_mp(src, dst, stage):
        @pl.loop(1, 16)
        def _(i):
            send(src, dst, stage, (d, c, (m + i) % 16))

    def to_dp(src, dst, stage):
        @pl.loop(1, 8)
        def _(i):
            send(src, dst, stage, ((d + i) % 8, c, m))

    def to_dp_both(src, dst, stage):
        @pl.loop(1, 16)
        def _(i):
            k = (d * 2 + c + i) % 16
            send(src, dst, stage, (k // 2, k % 2, m))

    def to_z(src, dst, stage):
        @pl.loop(1, 8)
        def _(i):
            send(src, dst, stage, (d, c, ((z + i) % 8) * 2 + yh))

    def to_plane_both(src, dst, stage):
        @pl.loop(1, 32)
        def _(i):
            k = (p * 2 + c + i) % 32
            send(src, dst, stage, (k // 4, k % 2, z * 2 + k // 2 % 2))

    to_dp(feat, featg.at[d], A1)
    to_mp(feat.at[2], xr.at[c, d, m], T1)
    to_mp(tgain_hbm, tg.at[c, m], TG)

    start = ((d * 2 + c) * 16 + m) * VOC
    load_index.wait()

    @pl.loop(0, ROWS // 64)
    def _(i):
        rows = lax.broadcasted_iota(jnp.int32, (64, 128), 0) + (i * 64 + start)
        hit = rows == index[0:1, :]
        for k in range(1, 32):
            hit = hit | (rows == index[k : k + 1, :])
        hit = hit & (rows < start + VOC)
        mask[pl.ds(pl.multiple_of(i * 64, 64), 64), :] = hit.astype(F32)

    load_fc.wait()
    load_feat.wait()
    arrived(A1)
    load_high.wait()
    arrived(T1)
    other = d + 1 - 2 * (d % 2)
    send(xr.at[c, d], xr.at[c, d], TY, (other, c, m))
    for half in range(4):
        cols = slice(half * 256, half * 256 + 256)
        acc = jnp.dot(featg[:, 0].reshape(128, 256), fc[0, :, cols], preferred_element_type=F32)
        for j in (1, 2):
            acc += jnp.dot(featg[:, j].reshape(128, 256), fc[j, :, cols], preferred_element_type=F32)
        for zz in range(8):
            part[half // 2, zz * 2 + half % 2] = acc[zz * 16 : zz * 16 + 16]
    send(part.at[1 - c], brecv0, B0, sib)

    arrived(TY)
    pair = xr.at[c, pl.ds(d - d % 2, 2)]

    @pl.loop(1, 4)
    def _(i):
        send(pair, pair, TX, ((d + 2 * i) % 8, c, m))

    arrived(B0)
    bsum[...] = part[c] + brecv0[...]

    @pl.loop(1, 16)
    def _(i):
        k = (m + i) % 16
        send(bsum.at[k], brecv1.at[m], B1, (d, c, k))

    brecv1[m] = bsum[m]
    arrived(B1)
    js = brecv1[0]
    for k in range(1, 16):
        js += brecv1[k]
    joined[...] = js

    eye = lax.broadcasted_iota(jnp.int32, (16, 128), 0) == lax.broadcasted_iota(jnp.int32, (16, 128), 1)

    def as_row(x):
        return jnp.sum(jnp.where(eye, jnp.sum(x, axis=1, keepdims=True), 0.0), axis=0, keepdims=True)

    def as_column(ref):
        return jnp.sum(jnp.where(eye, jnp.sum(ref[...], axis=0), 0.0), axis=1, keepdims=True)

    sq_s[...] = as_row(js * js)
    to_plane_both(sq_s, sq_r.at[p * 2 + c], S1)
    sq_r[p * 2 + c] = sq_s[...]
    arrived(S1)
    dscale = lax.rsqrt(as_column(sq_r) / D + EPS)
    load_dg.wait()
    own_cols = pl.multiple_of((c * 2 + yh) * 256, 256)
    gain = dgain[:, pl.ds(own_cols, 256)]
    xd[c, p, z] = (js * dscale * gain).astype(BF16)
    to_z(xd.at[c, p, z], xd.at[c, p, z], C1)

    arrived(TX)
    send(xr.at[c], xr.at[c], T3, sib)
    load_tg.wait()
    arrived(TG)
    send(tg.at[c], tg.at[c], TGS, sib)

    arrived(C1)

    def c2(i):
        q = (p + i) % 16
        return pltpu.make_async_remote_copy(
            src_ref=xd.at[c, p], dst_ref=xd.at[c, p], send_sem=c2s, recv_sem=c2r.at[p],
            device_id=(q // 2, c, z * 2 + q % 2), device_id_type=MESH,
        )

    def c3(q):
        return pltpu.make_async_remote_copy(
            src_ref=xd.at[c, q], dst_ref=xd.at[c, q], send_sem=c3s, recv_sem=c3r,
            device_id=sib, device_id_type=MESH,
        )

    @pl.loop(1, 16)
    def _(i):
        c2(i).start()

    c3(p).start()

    arrived(T3)
    arrived(TGS)

    def add_squares(i, acc):
        x = xr[i // 16, :, i % 16].reshape(128, 256).astype(F32)
        x = x * x
        return acc + x[:, :128] + x[:, 128:]

    squares = lax.fori_loop(0, 32, add_squares, jnp.zeros((128, 128), F32))
    tscale = lax.rsqrt(jnp.sum(squares, axis=1, keepdims=True) / D + EPS)

    load_head.wait()
    lt[...] = jnp.zeros_like(lt)

    @pl.loop(0, 8)
    def _(i):
        cc = i // 4
        mm = (i % 4) * 4
        x = jnp.concatenate(
            [
                (xr[cc, :, mm + k].reshape(128, 256).astype(F32) * tscale * tg[cc, mm + k]).astype(BF16)
                for k in range(4)
            ],
            axis=1,
        )
        cols = pl.ds(pl.multiple_of(i * 1024, 1024), 1024)
        lt[...] += lax.dot_general(head[:, cols], x, (((1,), (1,)), ((), ())), preferred_element_type=F32)

    on = mask[0:VOC, :] > 0.5
    logits = jnp.where(on, lt[...], LOW)
    tmax = jnp.max(logits, axis=0, keepdims=True)
    away = logits - tmax
    e = jnp.where(on, jnp.exp(away), 0.0)
    tz = jnp.sum(e, axis=0, keepdims=True)
    tw = jnp.sum(jnp.where(on, e * away, 0.0), axis=0, keepdims=True)

    def rows_of(a, b, w):
        return jnp.concatenate([a, b, w, jnp.zeros((1, 128), F32)], axis=0)

    def merge_t(ref):
        a = ref[...]
        top = jnp.max(a[:, 0:1, :], axis=0)
        low = a[:, 0:1, :] - top[None]
        f = jnp.exp(low)
        zz = jnp.sum(f * a[:, 1:2, :], axis=0)
        ww = jnp.sum(f * (a[:, 2:3, :] + jnp.where(a[:, 1:2, :] > 0.0, low, 0.0) * a[:, 1:2, :]), axis=0)
        return top, zz, ww

    def merge_d(ref):
        a = ref[...]
        top = jnp.max(a[:, 0:1, :], axis=0)
        f = jnp.exp(a[:, 0:1, :] - top[None])
        return top, jnp.sum(f * a[:, 1:2, :], axis=0), jnp.sum(a[:, 2:3, :], axis=0)

    us1[...] = rows_of(tmax, tz, tw)
    to_mp(us1, ur1.at[m], U1)
    ur1[m] = us1[...]

    @pl.loop(1, 12)
    def _(i):
        q = (p + 16 - i) % 16
        pltpu.make_async_copy(xd.at[c, q], xd.at[c, q], c2r.at[q]).wait()
        c3(q).start()

    arrived(U1)
    us2[...] = rows_of(*merge_t(ur1))
    to_dp_both(us2, ur2.at[d * 2 + c], U2)
    ur2[d * 2 + c] = us2[...]

    @pl.loop(12, 16)
    def _(i):
        q = (p + 16 - i) % 16
        pltpu.make_async_copy(xd.at[c, q], xd.at[c, q], c2r.at[q]).wait()
        c3(q).start()

    pltpu.make_async_copy(xd.at[1 - c], xd.at[1 - c], c3r).wait()
    ld[...] = jnp.zeros_like(ld)

    @pl.loop(0, 8)
    def _(i):
        x = jnp.concatenate([xd[k // 2, i * 2 + k % 2].reshape(128, 256) for k in range(4)], axis=1)
        cols = pl.ds(pl.multiple_of(i * 1024, 1024), 1024)
        ld[...] += lax.dot_general(head[:, cols], x, (((1,), (1,)), ((), ())), preferred_element_type=F32)

    arrived(U2)
    tmax, tz, tw = merge_t(ur2)
    tp = jnp.where(mask[0:VOC, :] > 0.5, jnp.exp(jnp.minimum(lt[...] - tmax, 0.0)) / tz, 0.0)
    placed[...] = tp
    teach = tw / tz - jnp.log(tz)

    logits = ld[...]
    dmax = jnp.max(logits, axis=0, keepdims=True)
    dz = jnp.sum(jnp.exp(logits - dmax), axis=0, keepdims=True)
    dw = jnp.sum(tp * logits, axis=0, keepdims=True)
    vs1[...] = rows_of(dmax, dz, dw)
    to_mp(vs1, vr1.at[m], V1)
    vr1[m] = vs1[...]
    arrived(V1)
    vs2[...] = rows_of(*merge_d(vr1))
    to_dp_both(vs2, vr2.at[d * 2 + c], V2)
    vr2[d * 2 + c] = vs2[...]
    arrived(V2)
    dmax, dz, dw = merge_d(vr2)
    log_total = dmax + jnp.log(dz)
    loss = teach - dw + log_total
    loss_out[...] = pltpu.roll(jnp.broadcast_to(loss, (8, 128)), (128 - d * 16) % 128, 1)

    g = jnp.exp(ld[...] - log_total) - placed[...]
    grad[...] = jnp.zeros_like(grad)
    grad[0:VOC, :] = g
    grad_rows = jnp.transpose(grad[...])[:, 0:VOC].astype(BF16)

    def r0_copy(dd):
        return pltpu.make_async_remote_copy(
            src_ref=hb.at[1 - c, pl.ds(dd * 2, 2)], dst_ref=r0.at[pl.ds(dd * 2, 2)],
            send_sem=r0s, recv_sem=r0r.at[dd], device_id=sib, device_id_type=MESH,
        )

    def compute(dd):
        for k in range(4):
            cols = pl.ds(pl.multiple_of(dd * 1024 + k * 256, 256), 256)
            h = jnp.dot(grad_rows, head[:, cols], preferred_element_type=F32)
            hf[k // 2, dd * 2 + k % 2] = h
            hb[k // 2, dd * 2 + k % 2] = h.astype(BF16)
        r0_copy(dd).start()

    def add_up(dd):
        pltpu.make_async_copy(r0.at[pl.ds(dd * 2, 2)], r0.at[pl.ds(dd * 2, 2)], r0r.at[dd]).wait()
        for k in range(2):
            q = dd * 2 + k
            r1s[q] = (hf[c, q] + r0[q].astype(F32)).astype(BF16)

    def to_peer(q):
        send(r1s.at[q], r1r.at[p], R1, (q // 2, c, z * 2 + q % 2))

    compute((d + 1) % 8)

    @pl.loop(2, 9)
    def _(i):
        compute((d + i) % 8)
        dd = (d + i - 1) % 8
        add_up(dd)
        to_peer(dd * 2)
        to_peer(dd * 2 + 1)

    add_up(d)
    to_peer(d * 2 + 1 - yh)
    r1r[p] = r1s[p]
    arrived(R1)
    for zz in range(8):
        acc = r1r[0, zz * 16 : zz * 16 + 16].astype(F32)
        for k in range(1, 16):
            acc += r1r[k, zz * 16 : zz * 16 + 16].astype(F32)
        r2s[zz] = acc.astype(BF16)

    @pl.loop(1, 8)
    def _(i):
        zz = (z + i) % 8
        send(r2s.at[zz], r2r.at[z], R2, (d, c, zz * 2 + yh))

    r2r[z] = r2s[z]
    arrived(R2)
    hidden = r2r[0].astype(F32)
    for k in range(1, 8):
        hidden += r2r[k].astype(F32)

    js = joined[...]
    weighted = hidden * gain
    in_s[...] = as_row(weighted * js)
    to_plane_both(in_s, in_r.at[p * 2 + c], I1)
    in_r[p * 2 + c] = in_s[...]
    gp_s[...] = jnp.sum(hidden * js * dscale, axis=0, keepdims=True)
    to_mp(gp_s, gp_r.at[m], GM)
    gp_r[m] = gp_s[...]
    arrived(I1)
    inner = as_column(in_r)
    jg[c, m] = (dscale * weighted - js * (dscale * dscale * dscale * inner / D)).astype(BF16)
    to_mp(jg.at[c, m], jg.at[c, m], JM)
    arrived(GM)
    for k in range(2):
        acc = gp_r[k]
        for zz in range(1, 8):
            acc += gp_r[zz * 2 + k]
        gs_s[k] = acc
    send(gs_s, gs_r.at[c], GS, sib)
    gs_r[c] = gs_s[...]
    feat_out[...] = jnp.concatenate(
        [jnp.concatenate([featg[k, j : j + 1] for k in range(8)], axis=1) for j in range(3)], axis=0
    )
    arrived(GS)
    for k in range(4):
        gain_out[:, k * 256 : k * 256 + 256] = gs_r[k // 2, k % 2]
    arrived(JM)
    send(jg.at[c], jg.at[c], JS, sib)
    arrived(JS)
    for k in range(4):
        for zz in range(8):
            grad_out[zz * 16 : zz * 16 + 16, k * 256 : k * 256 + 256] = jg[k // 2, zz * 2 + k % 2]

    for stage in volume:
        sent(stage)
    pltpu.make_async_copy(xd.at[c, pl.ds(0, 15)], xd.at[c, pl.ds(0, 15)], c2s).wait()
    pltpu.make_async_copy(xd.at[c], xd.at[c], c3s).wait()
    pltpu.make_async_copy(r0, r0, r0s).wait()


def shards(features, fc_weight, head, draft_gain, target_gain, teacher_index):
    vmem = pl.BlockSpec(memory_space=pltpu.VMEM)
    hbm = pl.BlockSpec(memory_space=pl.ANY)
    V = pltpu.VMEM
    stat = [V((4, 128), F32), V((16, 4, 128), F32)] * 2
    feat_all, joined_grad, gain_grad, loss = pl.pallas_call(
        kernel,
        out_shape=(
            jax.ShapeDtypeStruct((3, 128, 256), BF16),
            jax.ShapeDtypeStruct((128, 1024), BF16),
            jax.ShapeDtypeStruct((1, 1024), F32),
            jax.ShapeDtypeStruct((8, 128), F32),
        ),
        in_specs=[hbm] * 6,
        out_specs=(vmem, vmem, vmem, vmem),
        scratch_shapes=[
            V((VOC, D), BF16),
            V((3, 256, 1024), BF16),
            V((8, 3, 16, 256), BF16),
            V((1, 1024), F32),
            V((32, 128), jnp.int32),
            V((2, 16, 16, 256), F32),
            V((16, 16, 256), F32),
            V((16, 16, 256), F32),
            V((16, 16, 256), F32),
            V((2, 8, 16, 16, 256), BF16),
            V((2, 16, 1, 256), F32),
            V((2, 16, 8, 16, 256), BF16),
            V((16, 256), F32),
            V((1, 128), F32),
            V((32, 1, 128), F32),
            V((ROWS, 128), F32),
            V((VOC, 128), F32),
            V((VOC, 128), F32),
            V((VOC, 128), F32),
            V((ROWS, 128), F32),
            *stat,
            *stat,
            V((2, 16, 128, 256), F32),
            V((2, 16, 128, 256), BF16),
            V((16, 128, 256), BF16),
            V((16, 128, 256), BF16),
            V((16, 128, 256), BF16),
            V((8, 16, 256), BF16),
            V((8, 16, 256), BF16),
            V((1, 128), F32),
            V((32, 1, 128), F32),
            V((1, 256), F32),
            V((16, 1, 256), F32),
            V((2, 1, 256), F32),
            V((2, 2, 1, 256), F32),
            V((2, 16, 16, 256), BF16),
            pltpu.SemaphoreType.DMA((7,)),
            pltpu.SemaphoreType.DMA((STAGES,)),
            pltpu.SemaphoreType.DMA((STAGES,)),
            pltpu.SemaphoreType.DMA,
            pltpu.SemaphoreType.DMA((16,)),
            pltpu.SemaphoreType.DMA,
            pltpu.SemaphoreType.DMA,
            pltpu.SemaphoreType.DMA,
            pltpu.SemaphoreType.DMA((8,)),
        ],
        compiler_params=pltpu.CompilerParams(
            collective_id=0, has_side_effects=True, vmem_limit_bytes=60 * 2**20
        ),
        cost_estimate=pl.CostEstimate(flops=3_600_000_000, bytes_accessed=12_000_000, transcendentals=200_000),
    )(features, fc_weight, head, draft_gain.reshape(1, 1024), target_gain.reshape(1, 256), teacher_index.T)
    weight_grad = jnp.einsum("jtf,tc->jfc", feat_all, joined_grad, preferred_element_type=F32)
    return (weight_grad.astype(BF16), gain_grad.reshape(1024), loss[0, :16])


def solution(mesh):
    return jax.shard_map(
        shards,
        mesh=mesh,
        in_specs=(
            P(None, "dp", ("section", "mp")),
            P(None, ("section", "mp"), "dp"),
            P(("dp", "section", "mp"), None),
            P("dp"),
            P(("section", "mp")),
            P(),
        ),
        out_specs=(P(None, ("section", "mp"), "dp"), P("dp"), P("dp")),
        check_vma=False,
    )
```

time: 130 us -> 119 us (0.915)
  Pallas kernels: 123 us -> 114 us
  local copies, waits for them, and re-layouts: 4.02 us -> 1.78 us
    pallas_call x1, Pallas kernels: 123 us -> 114 us  [shards(): pl.pallas_call(kernel, out_shape=(jax.ShapeDtypeStruct((3, 128, 256), BF1...]
    unnamed x8 -> x3, local copies, waits for them, and re-layouts: 3.51 us -> 0.6 us
where the time goes in v2:
time: 119 us
  Pallas kernels  114 us (96%)
  matrix products  2.79 us (2%)
  local copies, waits for them, and re-layouts  1.78 us (1%)
    pallas_call x1, Pallas kernels, shards(): pl.pallas_call(kernel, out_shape=(jax.ShapeDtypeStruct((3, 128, 256), BF1...  114 us
    dot_general x1, matrix products, shards(): jnp.einsum('jtf,tc->jfc', feat_all, joined_grad, preferred_element_type=F32)  2.79 us

profile of v2, /device:TPU:1, one launch (start us, length us, event | category | flops | bytes accessed | tf_op | source)
XLA Modules:
  0.0 119.3 jit_solution(6816490184982893334)
XLA Ops:
  0.6 114.1 %shard_map.85 = (bf16[3,128,256]{2,1,0:T(8,128)(2,1)}, bf16[128,1024]{1,0:T(8,128)(2,1)}, f32[1,1024]{1,0:T(1,128)}, f32[8,128]{1,0:T(8,128)}) custom-call(bf16[3,16,256]{2,1,0:T(8,128)(2,1)} %feat.1, bf16[3,256,1024]{2,1,0:T(8,128)(2,1)} %fc_hbm.1, bf16[501,8192]{1,0:T(8,128)(2,1)} %head_hbm.1, f32[1,1024]{1,0:T(1,128)} %bitcast.12, f32[1,256]{1,0:T(1,128)} %bitcast.13, ...), custom_call_target="tpu_custom_call" | custom-call | flops 3600000000 | bytes 12000000 | tf_op jit(solution)/shard_map/pallas_call | solution.py:422
  114.8 0.0 copy-start
  114.8 1.2 slice_bitcast_fusion
  116.0 2.8 %convolution_convert_fusion = bf16[3,256,1024]{2,1,0:T(8,128)(2,1)} fusion(bf16[3,128,256]{2,1,0:T(8,128)(2,1)} %get-tuple-element.7, bf16[128,1024]{1,0:T(8,128)(2,1)} %get-tuple-element.8), kind=kOutput, calls=%fused_computation | convolution fusion | flops 202113024 | bytes 2031616 | tf_op jit(solution)/shard_map/jtf,tc->jfc/dot_general | solution.py:484
  118.7 0.0 copy-done
  118.7 0.6 copy.12
Async XLA Ops:
  114.8 4.0 %copy-start = (f32[1,1024]{1,0:T(1,128)S(1)}, f32[1,1024]{1,0:T(1,128)}, u32[]{:S(2)}) copy-start(f32[1,1024]{1,0:T(1,128)} %get-tuple-element.9) | copy-start | bytes 12292

commit v3 on v2

--- a/solution.py
+++ b/solution.py
@@ -14,7 +14,7 @@
 BF16 = jnp.bfloat16
 MESH = pl.DeviceIdType.MESH
 
-(A1, T1, TG, TY, TX, T3, TGS, B0, B1, S1, C1, U1, U2, V1, V2, R1, R2, I1, GM, GS, JM, JS) = range(22)
+(A1, T1, TG, TY, TX, TX2, T3, TGS, B0, B1, S1, C1, U1, U2, V1, V2, R1, R2, GM, GS, JM, JS) = range(22)
 STAGES = 22
 
 
@@ -24,7 +24,7 @@
     head, fc, featg, dgain, index, part, brecv0, bsum, brecv1, xr, tg, xd, joined,
     sq_s, sq_r, mask, lt, ld, placed, grad,
     us1, ur1, us2, ur2, vs1, vr1, vs2, vr2,
-    hf, hb, r0, r1s, r1r, r2s, r2r, in_s, in_r, gp_s, gp_r, gs_s, gs_r, jg,
+    hf, hb, r0, r1s, r1r, r2s, r2r, gp_s, gp_r, gs_s, gs_r, jg,
     load_sem, ssem, rsem, c2s, c2r, c3s, c3r, r0s, r0r,
 ):
     d = lax.axis_index("dp")
@@ -69,10 +69,10 @@
 
     volume = {
         A1: featg.at[pl.ds(0, 7)], T1: xr.at[c, d, pl.ds(0, 15)], TG: tg.at[c, pl.ds(0, 15)], TY: xr.at[c, d],
-        TX: xr.at[c, pl.ds(0, 6)], T3: xr.at[c], TGS: tg.at[c], B0: brecv0, B1: bsum.at[pl.ds(0, 15)],
+        TX: xr.at[c, pl.ds(0, 6), pl.ds(0, 8)], TX2: xr.at[c, pl.ds(0, 6), pl.ds(0, 8)], T3: xr.at[c], TGS: tg.at[c], B0: brecv0, B1: bsum.at[pl.ds(0, 15)],
         S1: sq_r.at[pl.ds(0, 31)], C1: xd.at[c, p, pl.ds(0, 7)], U1: ur1.at[pl.ds(0, 15)], U2: ur2.at[pl.ds(0, 15)],
         V1: vr1.at[pl.ds(0, 15)], V2: vr2.at[pl.ds(0, 15)], R1: r1r.at[pl.ds(0, 15)], R2: r2r.at[pl.ds(0, 7)],
-        I1: in_r.at[pl.ds(0, 31)], GM: gp_r.at[pl.ds(0, 15)], GS: gs_s, JM: jg.at[c, pl.ds(0, 15)], JS: jg.at[c],
+        GM: gp_r.at[pl.ds(0, 15)], GS: gs_s, JM: jg.at[c, pl.ds(0, 15)], JS: jg.at[c],
     }
 
     def arrived(stage):
@@ -127,10 +127,6 @@
     load_fc.wait()
     load_feat.wait()
     arrived(A1)
-    load_high.wait()
-    arrived(T1)
-    other = d + 1 - 2 * (d % 2)
-    send(xr.at[c, d], xr.at[c, d], TY, (other, c, m))
     for half in range(4):
         cols = slice(half * 256, half * 256 + 256)
         acc = jnp.dot(featg[:, 0].reshape(128, 256), fc[0, :, cols], preferred_element_type=F32)
@@ -140,13 +136,6 @@
             part[half // 2, zz * 2 + half % 2] = acc[zz * 16 : zz * 16 + 16]
     send(part.at[1 - c], brecv0, B0, sib)
 
-    arrived(TY)
-    pair = xr.at[c, pl.ds(d - d % 2, 2)]
-
-    @pl.loop(1, 4)
-    def _(i):
-        send(pair, pair, TX, ((d + 2 * i) % 8, c, m))
-
     arrived(B0)
     bsum[...] = part[c] + brecv0[...]
 
@@ -156,6 +145,21 @@
         send(bsum.at[k], brecv1.at[m], B1, (d, c, k))
 
     brecv1[m] = bsum[m]
+
+    load_high.wait()
+    arrived(T1)
+    other = d + 1 - 2 * (d % 2)
+    send(xr.at[c, d], xr.at[c, d], TY, (other, c, m))
+    arrived(TY)
+
+    def along_x(first, stage):
+        pair = xr.at[c, pl.ds(d - d % 2, 2), pl.ds(first, 8)]
+
+        @pl.loop(1, 4)
+        def _(i):
+            send(pair, pair, stage, ((d + 2 * i) % 8, c, m))
+
+    along_x(0, TX)
     arrived(B1)
     js = brecv1[0]
     for k in range(1, 16):
@@ -181,8 +185,7 @@
     xd[c, p, z] = (js * dscale * gain).astype(BF16)
     to_z(xd.at[c, p, z], xd.at[c, p, z], C1)
 
-    arrived(TX)
-    send(xr.at[c], xr.at[c], T3, sib)
+    along_x(8, TX2)
     load_tg.wait()
     arrived(TG)
     send(tg.at[c], tg.at[c], TGS, sib)
@@ -207,6 +210,9 @@
         c2(i).start()
 
     c3(p).start()
+    arrived(TX)
+    arrived(TX2)
+    send(xr.at[c], xr.at[c], T3, sib)
 
     arrived(T3)
     arrived(TGS)
@@ -244,25 +250,19 @@
     tz = jnp.sum(e, axis=0, keepdims=True)
     tw = jnp.sum(jnp.where(on, e * away, 0.0), axis=0, keepdims=True)
 
-    def rows_of(a, b, w):
-        return jnp.concatenate([a, b, w, jnp.zeros((1, 128), F32)], axis=0)
-
-    def merge_t(ref):
+    def rows_of(*rows):
+        return jnp.concatenate(rows, axis=0)
+
+    def merge(ref):
         a = ref[...]
         top = jnp.max(a[:, 0:1, :], axis=0)
         low = a[:, 0:1, :] - top[None]
         f = jnp.exp(low)
         zz = jnp.sum(f * a[:, 1:2, :], axis=0)
         ww = jnp.sum(f * (a[:, 2:3, :] + jnp.where(a[:, 1:2, :] > 0.0, low, 0.0) * a[:, 1:2, :]), axis=0)
-        return top, zz, ww
-
-    def merge_d(ref):
-        a = ref[...]
-        top = jnp.max(a[:, 0:1, :], axis=0)
-        f = jnp.exp(a[:, 0:1, :] - top[None])
-        return top, jnp.sum(f * a[:, 1:2, :], axis=0), jnp.sum(a[:, 2:3, :], axis=0)
-
-    us1[...] = rows_of(tmax, tz, tw)
+        return top, zz, ww, jnp.sum(a[:, 3:4, :], axis=0)
+
+    us1[...] = rows_of(tmax, tz, tw, jnp.zeros_like(tw))
     to_mp(us1, ur1.at[m], U1)
     ur1[m] = us1[...]
 
@@ -273,7 +273,7 @@
         c3(q).start()
 
     arrived(U1)
-    us2[...] = rows_of(*merge_t(ur1))
+    us2[...] = rows_of(*merge(ur1))
     to_dp_both(us2, ur2.at[d * 2 + c], U2)
     ur2[d * 2 + c] = us2[...]
 
@@ -293,26 +293,30 @@
         ld[...] += lax.dot_general(head[:, cols], x, (((1,), (1,)), ((), ())), preferred_element_type=F32)
 
     arrived(U2)
-    tmax, tz, tw = merge_t(ur2)
+    tmax, tz, tw, _ = merge(ur2)
     tp = jnp.where(mask[0:VOC, :] > 0.5, jnp.exp(jnp.minimum(lt[...] - tmax, 0.0)) / tz, 0.0)
     placed[...] = tp
     teach = tw / tz - jnp.log(tz)
 
     logits = ld[...]
     dmax = jnp.max(logits, axis=0, keepdims=True)
-    dz = jnp.sum(jnp.exp(logits - dmax), axis=0, keepdims=True)
+    away = logits - dmax
+    e = jnp.exp(away)
+    dz = jnp.sum(e, axis=0, keepdims=True)
+    ds = jnp.sum(e * away, axis=0, keepdims=True)
     dw = jnp.sum(tp * logits, axis=0, keepdims=True)
-    vs1[...] = rows_of(dmax, dz, dw)
+    vs1[...] = rows_of(dmax, dz, ds, dw)
     to_mp(vs1, vr1.at[m], V1)
     vr1[m] = vs1[...]
     arrived(V1)
-    vs2[...] = rows_of(*merge_d(vr1))
+    vs2[...] = rows_of(*merge(vr1))
     to_dp_both(vs2, vr2.at[d * 2 + c], V2)
     vr2[d * 2 + c] = vs2[...]
     arrived(V2)
-    dmax, dz, dw = merge_d(vr2)
+    dmax, dz, ds, dw = merge(vr2)
     log_total = dmax + jnp.log(dz)
     loss = teach - dw + log_total
+    moment = ds / dz + (dmax - dw)
     loss_out[...] = pltpu.roll(jnp.broadcast_to(loss, (8, 128)), (128 - d * 16) % 128, 1)
 
     g = jnp.exp(ld[...] - log_total) - placed[...]
@@ -376,16 +380,13 @@
 
     js = joined[...]
     weighted = hidden * gain
-    in_s[...] = as_row(weighted * js)
-    to_plane_both(in_s, in_r.at[p * 2 + c], I1)
-    in_r[p * 2 + c] = in_s[...]
+    own_tokens = lax.broadcasted_iota(jnp.int32, (16, 128), 0) + z * 16 == lax.broadcasted_iota(jnp.int32, (16, 128), 1)
+    back = jnp.sum(jnp.where(own_tokens, moment, 0.0), axis=1, keepdims=True)
+    jg[c, m] = (dscale * weighted - js * (dscale * dscale * back / D)).astype(BF16)
+    to_mp(jg.at[c, m], jg.at[c, m], JM)
     gp_s[...] = jnp.sum(hidden * js * dscale, axis=0, keepdims=True)
     to_mp(gp_s, gp_r.at[m], GM)
     gp_r[m] = gp_s[...]
-    arrived(I1)
-    inner = as_column(in_r)
-    jg[c, m] = (dscale * weighted - js * (dscale * dscale * dscale * inner / D)).astype(BF16)
-    to_mp(jg.at[c, m], jg.at[c, m], JM)
     arrived(GM)
     for k in range(2):
         acc = gp_r[k]
@@ -459,8 +460,6 @@
             V((16, 128, 256), BF16),
             V((8, 16, 256), BF16),
             V((8, 16, 256), BF16),
-            V((1, 128), F32),
-            V((32, 1, 128), F32),
             V((1, 256), F32),
             V((16, 1, 256), F32),
             V((2, 1, 256), F32),

time: 119 us -> 115 us (0.966); the launches traced: 119 us -> 114 us
  Pallas kernels: 114 us -> 108 us
    pallas_call x1, Pallas kernels: 114 us -> 108 us  [shards(): pl.pallas_call(kernel, out_shape=(jax.ShapeDtypeStruct((3, 128, 256), BF1...]
where the time goes in v3:
time: 115 us; the launch traced here: 114 us
  Pallas kernels  108 us (94%)
  matrix products  2.79 us (2%)
  local copies, waits for them, and re-layouts  1.78 us (2%)
    pallas_call x1, Pallas kernels, shards(): pl.pallas_call(kernel, out_shape=(jax.ShapeDtypeStruct((3, 128, 256), BF1...  108 us
    dot_general x1, matrix products, shards(): jnp.einsum('jtf,tc->jfc', feat_all, joined_grad, preferred_element_type=F32)  2.79 us

profile of v3, /device:TPU:1, one launch (start us, length us, event | category | flops | bytes accessed | tf_op | source)
XLA Modules:
  0.0 113.6 jit_solution(14468237703504981448)
XLA Ops:
  0.6 108.4 %shard_map.85 = (bf16[3,128,256]{2,1,0:T(8,128)(2,1)}, bf16[128,1024]{1,0:T(8,128)(2,1)}, f32[1,1024]{1,0:T(1,128)}, f32[8,128]{1,0:T(8,128)}) custom-call(bf16[3,16,256]{2,1,0:T(8,128)(2,1)} %feat.1, bf16[3,256,1024]{2,1,0:T(8,128)(2,1)} %fc_hbm.1, bf16[501,8192]{1,0:T(8,128)(2,1)} %head_hbm.1, f32[1,1024]{1,0:T(1,128)} %bitcast.12, f32[1,256]{1,0:T(1,128)} %bitcast.13, ...), custom_call_target="tpu_custom_call" | custom-call | flops 3600000000 | bytes 12000000 | tf_op jit(solution)/shard_map/pallas_call | solution.py:423
  109.0 0.0 copy-start
  109.0 1.2 %slice_bitcast_fusion = f32[16]{0:T(128)} fusion(f32[8,128]{1,0:T(8,128)} %get-tuple-element.10), kind=kLoop, calls=%fused_computation.2 | loop fusion | bytes 128 | tf_op jit(solution)/shard_map/squeeze | solution.py:484
  110.2 2.8 %convolution_convert_fusion = bf16[3,256,1024]{2,1,0:T(8,128)(2,1)} fusion(bf16[3,128,256]{2,1,0:T(8,128)(2,1)} %get-tuple-element.7, bf16[128,1024]{1,0:T(8,128)(2,1)} %get-tuple-element.8), kind=kOutput, calls=%fused_computation | convolution fusion | flops 202113024 | bytes 2031616 | tf_op jit(solution)/shard_map/jtf,tc->jfc/dot_general | solution.py:483
  113.0 0.0 copy-done
  113.0 0.6 copy.12
Async XLA Ops:
  109.0 4.0 %copy-start = (f32[1,1024]{1,0:T(1,128)S(1)}, f32[1,1024]{1,0:T(1,128)}, u32[]{:S(2)}) copy-start(f32[1,1024]{1,0:T(1,128)} %get-tuple-element.9) | copy-start | bytes 12292

commit v4 on v3

--- a/solution.py
+++ b/solution.py
@@ -20,12 +20,12 @@
 
 def kernel(
     feat, fc_hbm, head_hbm, dgain_hbm, tgain_hbm, index_hbm,
-    feat_out, grad_out, gain_out, loss_out,
+    grad_out, gain_out, loss_out,
     head, fc, featg, dgain, index, part, brecv0, bsum, brecv1, xr, tg, xd, joined,
     sq_s, sq_r, mask, lt, ld, placed, grad,
     us1, ur1, us2, ur2, vs1, vr1, vs2, vr2,
-    hf, hb, r0, r1s, r1r, r2s, r2r, gp_s, gp_r, gs_s, gs_r, jg,
-    load_sem, ssem, rsem, c2s, c2r, c3s, c3r, r0s, r0r,
+    hf, hb, r0, r1s, r1r, r2s, r2r, gp_s, gp_r, gs_s, gs_r, jg, feat_t, wg,
+    load_sem, ssem, rsem, c2s, c2r, c3s, c3r, r0s, r0r, out_sem,
 ):
     d = lax.axis_index("dp")
     c = lax.axis_index("section")
@@ -81,31 +81,34 @@
     def sent(stage):
         pltpu.make_async_copy(volume[stage], volume[stage], ssem.at[stage]).wait()
 
+    def step(i, n):
+        return i % 2 * ((i + 1) // 2) + (1 - i % 2) * (n - i // 2)
+
     def to_mp(src, dst, stage):
         @pl.loop(1, 16)
         def _(i):
-            send(src, dst, stage, (d, c, (m + i) % 16))
+            send(src, dst, stage, (d, c, (m + step(i, 16)) % 16))
 
     def to_dp(src, dst, stage):
         @pl.loop(1, 8)
         def _(i):
-            send(src, dst, stage, ((d + i) % 8, c, m))
+            send(src, dst, stage, ((d + step(i, 8)) % 8, c, m))
 
     def to_dp_both(src, dst, stage):
         @pl.loop(1, 16)
         def _(i):
-            k = (d * 2 + c + i) % 16
+            k = (d * 2 + c + step(i, 16)) % 16
             send(src, dst, stage, (k // 2, k % 2, m))
 
     def to_z(src, dst, stage):
         @pl.loop(1, 8)
         def _(i):
-            send(src, dst, stage, (d, c, ((z + i) % 8) * 2 + yh))
+            send(src, dst, stage, (d, c, ((z + step(i, 8)) % 8) * 2 + yh))
 
     def to_plane_both(src, dst, stage):
         @pl.loop(1, 32)
         def _(i):
-            k = (p * 2 + c + i) % 32
+            k = (p * 2 + c + step(i, 32)) % 32
             send(src, dst, stage, (k // 4, k % 2, z * 2 + k // 2 % 2))
 
     to_dp(feat, featg.at[d], A1)
@@ -136,20 +139,21 @@
             part[half // 2, zz * 2 + half % 2] = acc[zz * 16 : zz * 16 + 16]
     send(part.at[1 - c], brecv0, B0, sib)
 
-    arrived(B0)
-    bsum[...] = part[c] + brecv0[...]
-
-    @pl.loop(1, 16)
-    def _(i):
-        k = (m + i) % 16
-        send(bsum.at[k], brecv1.at[m], B1, (d, c, k))
-
-    brecv1[m] = bsum[m]
-
     load_high.wait()
     arrived(T1)
     other = d + 1 - 2 * (d % 2)
     send(xr.at[c, d], xr.at[c, d], TY, (other, c, m))
+
+    arrived(B0)
+    bsum[...] = part[c] + brecv0[...]
+
+    @pl.loop(1, 16)
+    def _(i):
+        k = (m + step(i, 16)) % 16
+        send(bsum.at[k], brecv1.at[m], B1, (d, c, k))
+
+    brecv1[m] = bsum[m]
+
     arrived(TY)
 
     def along_x(first, stage):
@@ -193,7 +197,7 @@
     arrived(C1)
 
     def c2(i):
-        q = (p + i) % 16
+        q = (p + step(i, 16)) % 16
         return pltpu.make_async_remote_copy(
             src_ref=xd.at[c, p], dst_ref=xd.at[c, p], send_sem=c2s, recv_sem=c2r.at[p],
             device_id=(q // 2, c, z * 2 + q % 2), device_id_type=MESH,
@@ -268,7 +272,7 @@
 
     @pl.loop(1, 12)
     def _(i):
-        q = (p + 16 - i) % 16
+        q = (p + step(i, 16)) % 16
         pltpu.make_async_copy(xd.at[c, q], xd.at[c, q], c2r.at[q]).wait()
         c3(q).start()
 
@@ -279,7 +283,7 @@
 
     @pl.loop(12, 16)
     def _(i):
-        q = (p + 16 - i) % 16
+        q = (p + step(i, 16)) % 16
         pltpu.make_async_copy(xd.at[c, q], xd.at[c, q], c2r.at[q]).wait()
         c3(q).start()
 
@@ -317,7 +321,7 @@
     log_total = dmax + jnp.log(dz)
     loss = teach - dw + log_total
     moment = ds / dz + (dmax - dw)
-    loss_out[...] = pltpu.roll(jnp.broadcast_to(loss, (8, 128)), (128 - d * 16) % 128, 1)
+    loss_out[...] = pltpu.roll(jnp.broadcast_to(loss, (8, 128)), (128 - d * 16) % 128, 1)[0:1, 0:16]
 
     g = jnp.exp(ld[...] - log_total) - placed[...]
     grad[...] = jnp.zeros_like(grad)
@@ -351,8 +355,8 @@
 
     @pl.loop(2, 9)
     def _(i):
-        compute((d + i) % 8)
-        dd = (d + i - 1) % 8
+        compute((d + step(i, 8) * (1 - i // 8)) % 8)
+        dd = (d + step(i - 1, 8)) % 8
         add_up(dd)
         to_peer(dd * 2)
         to_peer(dd * 2 + 1)
@@ -369,7 +373,7 @@
 
     @pl.loop(1, 8)
     def _(i):
-        zz = (z + i) % 8
+        zz = (z + step(i, 8)) % 8
         send(r2s.at[zz], r2r.at[z], R2, (d, c, zz * 2 + yh))
 
     r2r[z] = r2s[z]
@@ -387,6 +391,21 @@
     gp_s[...] = jnp.sum(hidden * js * dscale, axis=0, keepdims=True)
     to_mp(gp_s, gp_r.at[m], GM)
     gp_r[m] = gp_s[...]
+    for j in range(3):
+        feat_t[j] = jnp.transpose(featg[:, j].reshape(128, 256).astype(F32)).astype(BF16)
+    arrived(JM)
+    send(jg.at[c], jg.at[c], JS, sib)
+
+    def weight_grad(cc):
+        cols = pl.ds(pl.multiple_of(cc * 512, 512), 512)
+        for k in range(2):
+            rows = jnp.concatenate([jg[cc, zz * 2 + k] for zz in range(8)], axis=0)
+            part_cols = pl.ds(pl.multiple_of(cc * 512 + k * 256, 256), 256)
+            for j in range(3):
+                wg[j, :, part_cols] = jnp.dot(feat_t[j], rows, preferred_element_type=F32).astype(BF16)
+        return pltpu.make_async_copy(wg.at[:, :, cols], grad_out.at[:, :, cols], out_sem.at[cc])
+
+    weight_grad(c).start()
     arrived(GM)
     for k in range(2):
         acc = gp_r[k]
@@ -395,18 +414,14 @@
         gs_s[k] = acc
     send(gs_s, gs_r.at[c], GS, sib)
     gs_r[c] = gs_s[...]
-    feat_out[...] = jnp.concatenate(
-        [jnp.concatenate([featg[k, j : j + 1] for k in range(8)], axis=1) for j in range(3)], axis=0
-    )
+    arrived(JS)
+    weight_grad(1 - c).start()
     arrived(GS)
     for k in range(4):
         gain_out[:, k * 256 : k * 256 + 256] = gs_r[k // 2, k % 2]
-    arrived(JM)
-    send(jg.at[c], jg.at[c], JS, sib)
-    arrived(JS)
-    for k in range(4):
-        for zz in range(8):
-            grad_out[zz * 16 : zz * 16 + 16, k * 256 : k * 256 + 256] = jg[k // 2, zz * 2 + k % 2]
+    for k in range(2):
+        half = slice(k * 512, k * 512 + 512)
+        pltpu.make_async_copy(wg.at[:, :, half], grad_out.at[:, :, half], out_sem.at[k]).wait()
 
     for stage in volume:
         sent(stage)
@@ -420,16 +435,15 @@
     hbm = pl.BlockSpec(memory_space=pl.ANY)
     V = pltpu.VMEM
     stat = [V((4, 128), F32), V((16, 4, 128), F32)] * 2
-    feat_all, joined_grad, gain_grad, loss = pl.pallas_call(
+    weight_grad, gain_grad, loss = pl.pallas_call(
         kernel,
         out_shape=(
-            jax.ShapeDtypeStruct((3, 128, 256), BF16),
-            jax.ShapeDtypeStruct((128, 1024), BF16),
+            jax.ShapeDtypeStruct((3, 256, 1024), BF16),
             jax.ShapeDtypeStruct((1, 1024), F32),
-            jax.ShapeDtypeStruct((8, 128), F32),
+            jax.ShapeDtypeStruct((1, 16), F32),
         ),
         in_specs=[hbm] * 6,
-        out_specs=(vmem, vmem, vmem, vmem),
+        out_specs=(hbm, vmem, vmem),
         scratch_shapes=[
             V((VOC, D), BF16),
             V((3, 256, 1024), BF16),
@@ -465,6 +479,8 @@
             V((2, 1, 256), F32),
             V((2, 2, 1, 256), F32),
             V((2, 16, 16, 256), BF16),
+            V((3, 256, 128), BF16),
+            V((3, 256, 1024), BF16),
             pltpu.SemaphoreType.DMA((7,)),
             pltpu.SemaphoreType.DMA((STAGES,)),
             pltpu.SemaphoreType.DMA((STAGES,)),
@@ -474,14 +490,14 @@
             pltpu.SemaphoreType.DMA,
             pltpu.SemaphoreType.DMA,
             pltpu.SemaphoreType.DMA((8,)),
+            pltpu.SemaphoreType.DMA((2,)),
         ],
         compiler_params=pltpu.CompilerParams(
             collective_id=0, has_side_effects=True, vmem_limit_bytes=60 * 2**20
         ),
         cost_estimate=pl.CostEstimate(flops=3_600_000_000, bytes_accessed=12_000_000, transcendentals=200_000),
     )(features, fc_weight, head, draft_gain.reshape(1, 1024), target_gain.reshape(1, 256), teacher_index.T)
-    weight_grad = jnp.einsum("jtf,tc->jfc", feat_all, joined_grad, preferred_element_type=F32)
-    return (weight_grad.astype(BF16), gain_grad.reshape(1024), loss[0, :16])
+    return (weight_grad, gain_grad.reshape(1024), loss.reshape(16))
 
 
 def solution(mesh):

time: 115 us -> 111 us (0.965)
  matrix products: 2.79 us -> 0 us
  Pallas kernels: 108 us -> 106 us
  local copies, waits for them, and re-layouts: 1.78 us -> 3.78 us
    unnamed x3 -> x7, local copies, waits for them, and re-layouts: 0.6 us -> 3.78 us
    dot_general x1 -> x0, matrix products: 2.79 us -> none  [shards(): jnp.einsum('jtf,tc->jfc', feat_all, joined_grad, preferred_element_type=F32)]
    pallas_call x1, Pallas kernels: 108 us -> 106 us  [shards(): pl.pallas_call(kernel, out_shape=(jax.ShapeDtypeStruct((3, 256, 1024), BF...]
    squeeze x1 -> x0, local copies, waits for them, and re-layouts: 1.19 us -> none  [shards(): return (weight_grad.astype(BF16), gain_grad.reshape(1024), loss[0, :16])]
where the time goes in v4:
time: 111 us
  Pallas kernels  106 us (95%)
  local copies, waits for them, and re-layouts  3.78 us (3%)
    pallas_call x1, Pallas kernels, shards(): pl.pallas_call(kernel, out_shape=(jax.ShapeDtypeStruct((3, 256, 1024), BF...  106 us
    unnamed x7, local copies, waits for them, and re-layouts  3.78 us

profile of v4, /device:TPU:1, one launch (start us, length us, event | category | flops | bytes accessed | tf_op | source)
XLA Modules:
  0.0 110.7 jit_solution(17434122945237121291)
XLA Ops:
  0.6 106.3 %shard_map.85 = (bf16[3,256,1024]{2,1,0:T(8,128)(2,1)}, f32[1,1024]{1,0:T(1,128)}, f32[1,16]{1,0:T(1,128)}) custom-call(bf16[3,16,256]{2,1,0:T(8,128)(2,1)} %feat.1, bf16[3,256,1024]{2,1,0:T(8,128)(2,1)} %fc_hbm.1, bf16[501,8192]{1,0:T(8,128)(2,1)} %head_hbm.1, f32[1,1024]{1,0:T(1,128)} %bitcast.7, f32[1,256]{1,0:T(1,128)} %bitcast.8, s32[32,128]{1,0:T(8,128)} %bitcast.6), custom_call_target="tpu_custom_call" | custom-call | flops 3600000000 | bytes 12000000 | tf_op jit(solution)/shard_map/pallas_call | solution.py:438
  106.9 0.0 copy-start
  106.9 0.0 copy-start.1
  106.9 2.7 %copy.12 = bf16[3,256,1024]{2,1,0:T(8,128)(2,1)} copy(bf16[3,256,1024]{2,1,0:T(8,128)(2,1)} %get-tuple-element.12) | data formatting | bytes 3145728
  109.6 0.0 copy-done
  109.6 0.6 copy.13
  110.2 0.0 copy-done.1
  110.2 0.5 copy.14
Async XLA Ops:
  106.9 2.7 %copy-start = (f32[1,1024]{1,0:T(1,128)S(1)}, f32[1,1024]{1,0:T(1,128)}, u32[]{:S(2)}) copy-start(f32[1,1024]{1,0:T(1,128)} %get-tuple-element.7) | copy-start | bytes 12292
  106.9 3.3 %copy-start.1 = (f32[1,16]{1,0:T(1,128)S(1)}, f32[1,16]{1,0:T(1,128)}, u32[]{:S(2)}) copy-start(f32[1,16]{1,0:T(1,128)} %get-tuple-element.8) | copy-start | bytes 196

commit v5 on v4

--- a/solution.py
+++ b/solution.py
@@ -14,8 +14,8 @@
 BF16 = jnp.bfloat16
 MESH = pl.DeviceIdType.MESH
 
-(A1, T1, TG, TY, TX, TX2, T3, TGS, B0, B1, S1, C1, U1, U2, V1, V2, R1, R2, GM, GS, JM, JS) = range(22)
-STAGES = 22
+(A1, T1, TG, TY, TX, TX2, T3, TGS, B0, B1, S1, C1, U1, U2, V1, V2, W1, W2, R1, R2, GM, GS, JM, JS) = range(24)
+STAGES = 24
 
 
 def kernel(
@@ -23,7 +23,7 @@
     grad_out, gain_out, loss_out,
     head, fc, featg, dgain, index, part, brecv0, bsum, brecv1, xr, tg, xd, joined,
     sq_s, sq_r, mask, lt, ld, placed, grad,
-    us1, ur1, us2, ur2, vs1, vr1, vs2, vr2,
+    us1, ur1, us2, ur2, vs1, vr1, vs2, vr2, ws1, wr1, ws2, wr2,
     hf, hb, r0, r1s, r1r, r2s, r2r, gp_s, gp_r, gs_s, gs_r, jg, feat_t, wg,
     load_sem, ssem, rsem, c2s, c2r, c3s, c3r, r0s, r0r, out_sem,
 ):
@@ -71,7 +71,7 @@
         A1: featg.at[pl.ds(0, 7)], T1: xr.at[c, d, pl.ds(0, 15)], TG: tg.at[c, pl.ds(0, 15)], TY: xr.at[c, d],
         TX: xr.at[c, pl.ds(0, 6), pl.ds(0, 8)], TX2: xr.at[c, pl.ds(0, 6), pl.ds(0, 8)], T3: xr.at[c], TGS: tg.at[c], B0: brecv0, B1: bsum.at[pl.ds(0, 15)],
         S1: sq_r.at[pl.ds(0, 31)], C1: xd.at[c, p, pl.ds(0, 7)], U1: ur1.at[pl.ds(0, 15)], U2: ur2.at[pl.ds(0, 15)],
-        V1: vr1.at[pl.ds(0, 15)], V2: vr2.at[pl.ds(0, 15)], R1: r1r.at[pl.ds(0, 15)], R2: r2r.at[pl.ds(0, 7)],
+        W1: wr1.at[pl.ds(0, 15)], W2: wr2.at[pl.ds(0, 15)], V1: vr1.at[pl.ds(0, 15)], V2: vr2.at[pl.ds(0, 15)], R1: r1r.at[pl.ds(0, 15)], R2: r2r.at[pl.ds(0, 7)],
         GM: gp_r.at[pl.ds(0, 15)], GS: gs_s, JM: jg.at[c, pl.ds(0, 15)], JS: jg.at[c],
     }
 
@@ -254,8 +254,8 @@
     tz = jnp.sum(e, axis=0, keepdims=True)
     tw = jnp.sum(jnp.where(on, e * away, 0.0), axis=0, keepdims=True)
 
-    def rows_of(*rows):
-        return jnp.concatenate(rows, axis=0)
+    def rows_of(a, b, w):
+        return jnp.concatenate([a, b, w, jnp.zeros((1, 128), F32)], axis=0)
 
     def merge(ref):
         a = ref[...]
@@ -264,29 +264,18 @@
         f = jnp.exp(low)
         zz = jnp.sum(f * a[:, 1:2, :], axis=0)
         ww = jnp.sum(f * (a[:, 2:3, :] + jnp.where(a[:, 1:2, :] > 0.0, low, 0.0) * a[:, 1:2, :]), axis=0)
-        return top, zz, ww, jnp.sum(a[:, 3:4, :], axis=0)
-
-    us1[...] = rows_of(tmax, tz, tw, jnp.zeros_like(tw))
+        return top, zz, ww
+
+    us1[...] = rows_of(tmax, tz, tw)
     to_mp(us1, ur1.at[m], U1)
     ur1[m] = us1[...]
 
-    @pl.loop(1, 12)
+    @pl.loop(1, 16)
     def _(i):
         q = (p + step(i, 16)) % 16
         pltpu.make_async_copy(xd.at[c, q], xd.at[c, q], c2r.at[q]).wait()
         c3(q).start()
 
-    arrived(U1)
-    us2[...] = rows_of(*merge(ur1))
-    to_dp_both(us2, ur2.at[d * 2 + c], U2)
-    ur2[d * 2 + c] = us2[...]
-
-    @pl.loop(12, 16)
-    def _(i):
-        q = (p + step(i, 16)) % 16
-        pltpu.make_async_copy(xd.at[c, q], xd.at[c, q], c2r.at[q]).wait()
-        c3(q).start()
-
     pltpu.make_async_copy(xd.at[1 - c], xd.at[1 - c], c3r).wait()
     ld[...] = jnp.zeros_like(ld)
 
@@ -295,12 +284,6 @@
         x = jnp.concatenate([xd[k // 2, i * 2 + k % 2].reshape(128, 256) for k in range(4)], axis=1)
         cols = pl.ds(pl.multiple_of(i * 1024, 1024), 1024)
         ld[...] += lax.dot_general(head[:, cols], x, (((1,), (1,)), ((), ())), preferred_element_type=F32)
-
-    arrived(U2)
-    tmax, tz, tw, _ = merge(ur2)
-    tp = jnp.where(mask[0:VOC, :] > 0.5, jnp.exp(jnp.minimum(lt[...] - tmax, 0.0)) / tz, 0.0)
-    placed[...] = tp
-    teach = tw / tz - jnp.log(tz)
 
     logits = ld[...]
     dmax = jnp.max(logits, axis=0, keepdims=True)
@@ -308,21 +291,32 @@
     e = jnp.exp(away)
     dz = jnp.sum(e, axis=0, keepdims=True)
     ds = jnp.sum(e * away, axis=0, keepdims=True)
-    dw = jnp.sum(tp * logits, axis=0, keepdims=True)
-    vs1[...] = rows_of(dmax, dz, ds, dw)
+    vs1[...] = rows_of(dmax, dz, ds)
     to_mp(vs1, vr1.at[m], V1)
     vr1[m] = vs1[...]
+
+    arrived(U1)
+    us2[...] = rows_of(*merge(ur1))
+    to_dp_both(us2, ur2.at[d * 2 + c], U2)
+    ur2[d * 2 + c] = us2[...]
+
     arrived(V1)
     vs2[...] = rows_of(*merge(vr1))
     to_dp_both(vs2, vr2.at[d * 2 + c], V2)
     vr2[d * 2 + c] = vs2[...]
+
+    arrived(U2)
+    tmax, tz, tw = merge(ur2)
+    tp = jnp.where(mask[0:VOC, :] > 0.5, jnp.exp(jnp.minimum(lt[...] - tmax, 0.0)) / tz, 0.0)
+    placed[...] = tp
+    teach = tw / tz - jnp.log(tz)
+    ws1[...] = jnp.sum(tp * ld[...], axis=0, keepdims=True)
+    to_mp(ws1, wr1.at[m], W1)
+    wr1[m] = ws1[...]
+
     arrived(V2)
-    dmax, dz, ds, dw = merge(vr2)
+    dmax, dz, ds = merge(vr2)
     log_total = dmax + jnp.log(dz)
-    loss = teach - dw + log_total
-    moment = ds / dz + (dmax - dw)
-    loss_out[...] = pltpu.roll(jnp.broadcast_to(loss, (8, 128)), (128 - d * 16) % 128, 1)[0:1, 0:16]
-
     g = jnp.exp(ld[...] - log_total) - placed[...]
     grad[...] = jnp.zeros_like(grad)
     grad[0:VOC, :] = g
@@ -364,6 +358,10 @@
     add_up(d)
     to_peer(d * 2 + 1 - yh)
     r1r[p] = r1s[p]
+    arrived(W1)
+    ws2[...] = jnp.sum(wr1[...], axis=0)
+    to_dp_both(ws2, wr2.at[d * 2 + c], W2)
+    wr2[d * 2 + c] = ws2[...]
     arrived(R1)
     for zz in range(8):
         acc = r1r[0, zz * 16 : zz * 16 + 16].astype(F32)
@@ -377,6 +375,12 @@
         send(r2s.at[zz], r2r.at[z], R2, (d, c, zz * 2 + yh))
 
     r2r[z] = r2s[z]
+    arrived(W2)
+    dw = jnp.sum(wr2[...], axis=0)
+    loss = teach - dw + log_total
+    moment = ds / dz + (dmax - dw)
+    loss_out[...] = pltpu.roll(jnp.broadcast_to(loss, (8, 128)), (128 - d * 16) % 128, 1)[0:1, 0:16]
+
     arrived(R2)
     hidden = r2r[0].astype(F32)
     for k in range(1, 8):
@@ -467,6 +471,7 @@
             V((ROWS, 128), F32),
             *stat,
             *stat,
+            V((1, 128), F32), V((16, 1, 128), F32), V((1, 128), F32), V((16, 1, 128), F32),
             V((2, 16, 128, 256), F32),
             V((2, 16, 128, 256), BF16),
             V((16, 128, 256), BF16),

time: 111 us -> 111 us (level)
  no operation moved by 1% of the time
where the time goes in v5:
time: 111 us
  Pallas kernels  106 us (95%)
  local copies, waits for them, and re-layouts  3.78 us (3%)
    pallas_call x1, Pallas kernels, shards(): pl.pallas_call(kernel, out_shape=(jax.ShapeDtypeStruct((3, 256, 1024), BF...  106 us
    unnamed x7, local copies, waits for them, and re-layouts  3.78 us

profile of v5, /device:TPU:1, one launch (start us, length us, event | category | flops | bytes accessed | tf_op | source)
XLA Modules:
  0.0 110.8 jit_solution(2604541819439063221)
XLA Ops:
  0.6 106.3 %shard_map.85 = (bf16[3,256,1024]{2,1,0:T(8,128)(2,1)}, f32[1,1024]{1,0:T(1,128)}, f32[1,16]{1,0:T(1,128)}) custom-call(bf16[3,16,256]{2,1,0:T(8,128)(2,1)} %feat.1, bf16[3,256,1024]{2,1,0:T(8,128)(2,1)} %fc_hbm.1, bf16[501,8192]{1,0:T(8,128)(2,1)} %head_hbm.1, f32[1,1024]{1,0:T(1,128)} %bitcast.7, f32[1,256]{1,0:T(1,128)} %bitcast.8, s32[32,128]{1,0:T(8,128)} %bitcast.6), custom_call_target="tpu_custom_call" | custom-call | flops 3600000000 | bytes 12000000 | tf_op jit(solution)/shard_map/pallas_call | solution.py:442
  107.0 0.0 copy-start
  107.0 0.0 copy-start.1
  107.0 2.7 %copy.12 = bf16[3,256,1024]{2,1,0:T(8,128)(2,1)} copy(bf16[3,256,1024]{2,1,0:T(8,128)(2,1)} %get-tuple-element.12) | data formatting | bytes 3145728
  109.7 0.0 copy-done
  109.7 0.6 copy.13
  110.3 0.0 copy-done.1
  110.3 0.5 copy.14
Async XLA Ops:
  107.0 2.7 %copy-start = (f32[1,1024]{1,0:T(1,128)S(1)}, f32[1,1024]{1,0:T(1,128)}, u32[]{:S(2)}) copy-start(f32[1,1024]{1,0:T(1,128)} %get-tuple-element.7) | copy-start | bytes 12292
  107.0 3.3 %copy-start.1 = (f32[1,16]{1,0:T(1,128)S(1)}, f32[1,16]{1,0:T(1,128)}, u32[]{:S(2)}) copy-start(f32[1,16]{1,0:T(1,128)} %get-tuple-element.8) | copy-start | bytes 196

commit v6 on v5

--- a/solution.py
+++ b/solution.py
@@ -59,7 +59,13 @@
             barrier, inc=1, device_id=(k // 4, k % 2, z * 2 + k // 2 % 2), device_id_type=MESH
         )
 
-    pl.semaphore_wait(barrier, 46)
+    other = d + 1 - 2 * (d % 2)
+
+    @pl.loop(0, 16)
+    def _(i):
+        pl.semaphore_signal(barrier, inc=1, device_id=(other, c, (m + i) % 16), device_id_type=MESH)
+
+    pl.semaphore_wait(barrier, 62)
 
     def send(src, dst, stage, dev):
         pltpu.make_async_remote_copy(
@@ -69,7 +75,8 @@
 
     volume = {
         A1: featg.at[pl.ds(0, 7)], T1: xr.at[c, d, pl.ds(0, 15)], TG: tg.at[c, pl.ds(0, 15)], TY: xr.at[c, d],
-        TX: xr.at[c, pl.ds(0, 6), pl.ds(0, 8)], TX2: xr.at[c, pl.ds(0, 6), pl.ds(0, 8)], T3: xr.at[c], TGS: tg.at[c], B0: brecv0, B1: bsum.at[pl.ds(0, 15)],
+        TX: xr.at[c, pl.ds(0, 6), pl.ds(0, 10)],
+        TX2: xr.at[c, pl.ds(0, 6), pl.ds(0, 6)], T3: xr.at[c], TGS: tg.at[c], B0: brecv0, B1: bsum.at[pl.ds(0, 15)],
         S1: sq_r.at[pl.ds(0, 31)], C1: xd.at[c, p, pl.ds(0, 7)], U1: ur1.at[pl.ds(0, 15)], U2: ur2.at[pl.ds(0, 15)],
         W1: wr1.at[pl.ds(0, 15)], W2: wr2.at[pl.ds(0, 15)], V1: vr1.at[pl.ds(0, 15)], V2: vr2.at[pl.ds(0, 15)], R1: r1r.at[pl.ds(0, 15)], R2: r2r.at[pl.ds(0, 7)],
         GM: gp_r.at[pl.ds(0, 15)], GS: gs_s, JM: jg.at[c, pl.ds(0, 15)], JS: jg.at[c],
@@ -113,6 +120,11 @@
 
     to_dp(feat, featg.at[d], A1)
     to_mp(feat.at[2], xr.at[c, d, m], T1)
+
+    @pl.loop(0, 16)
+    def _(i):
+        send(feat.at[2], xr.at[c, d, m], TY, (other, c, (m + step(i, 16)) % 16))
+
     to_mp(tgain_hbm, tg.at[c, m], TG)
 
     start = ((d * 2 + c) * 16 + m) * VOC
@@ -139,31 +151,28 @@
             part[half // 2, zz * 2 + half % 2] = acc[zz * 16 : zz * 16 + 16]
     send(part.at[1 - c], brecv0, B0, sib)
 
+    arrived(B0)
+    bsum[...] = part[c] + brecv0[...]
+
+    @pl.loop(1, 16)
+    def _(i):
+        k = (m + step(i, 16)) % 16
+        send(bsum.at[k], brecv1.at[m], B1, (d, c, k))
+
+    brecv1[m] = bsum[m]
+
     load_high.wait()
     arrived(T1)
-    other = d + 1 - 2 * (d % 2)
-    send(xr.at[c, d], xr.at[c, d], TY, (other, c, m))
-
-    arrived(B0)
-    bsum[...] = part[c] + brecv0[...]
-
-    @pl.loop(1, 16)
-    def _(i):
-        k = (m + step(i, 16)) % 16
-        send(bsum.at[k], brecv1.at[m], B1, (d, c, k))
-
-    brecv1[m] = bsum[m]
-
     arrived(TY)
 
-    def along_x(first, stage):
-        pair = xr.at[c, pl.ds(d - d % 2, 2), pl.ds(first, 8)]
+    def along_x(first, count, stage):
+        pair = xr.at[c, pl.ds(d - d % 2, 2), pl.ds(first, count)]
 
         @pl.loop(1, 4)
         def _(i):
             send(pair, pair, stage, ((d + 2 * i) % 8, c, m))
 
-    along_x(0, TX)
+    along_x(0, 10, TX)
     arrived(B1)
     js = brecv1[0]
     for k in range(1, 16):
@@ -181,6 +190,7 @@
     sq_s[...] = as_row(js * js)
     to_plane_both(sq_s, sq_r.at[p * 2 + c], S1)
     sq_r[p * 2 + c] = sq_s[...]
+    along_x(10, 6, TX2)
     arrived(S1)
     dscale = lax.rsqrt(as_column(sq_r) / D + EPS)
     load_dg.wait()
@@ -189,7 +199,6 @@
     xd[c, p, z] = (js * dscale * gain).astype(BF16)
     to_z(xd.at[c, p, z], xd.at[c, p, z], C1)
 
-    along_x(8, TX2)
     load_tg.wait()
     arrived(TG)
     send(tg.at[c], tg.at[c], TGS, sib)

time: 111 us -> 107 us (0.964)
  Pallas kernels: 106 us -> 102 us
    pallas_call x1, Pallas kernels: 106 us -> 102 us  [shards(): pl.pallas_call(kernel, out_shape=(jax.ShapeDtypeStruct((3, 256, 1024), BF...]
where the time goes in v6:
time: 107 us; the launch traced here: 106 us
  Pallas kernels  102 us (95%)
  local copies, waits for them, and re-layouts  3.78 us (4%)
    pallas_call x1, Pallas kernels, shards(): pl.pallas_call(kernel, out_shape=(jax.ShapeDtypeStruct((3, 256, 1024), BF...  102 us
    unnamed x7, local copies, waits for them, and re-layouts  3.78 us

profile of v6, /device:TPU:1, one launch (start us, length us, event | category | flops | bytes accessed | tf_op | source)
XLA Modules:
  0.0 106.4 jit_solution(1193267702780747257)
XLA Ops:
  0.6 102.0 %shard_map.85 = (bf16[3,256,1024]{2,1,0:T(8,128)(2,1)}, f32[1,1024]{1,0:T(1,128)}, f32[1,16]{1,0:T(1,128)}) custom-call(bf16[3,16,256]{2,1,0:T(8,128)(2,1)} %feat.1, bf16[3,256,1024]{2,1,0:T(8,128)(2,1)} %fc_hbm.1, bf16[501,8192]{1,0:T(8,128)(2,1)} %head_hbm.1, f32[1,1024]{1,0:T(1,128)} %bitcast.7, f32[1,256]{1,0:T(1,128)} %bitcast.8, s32[32,128]{1,0:T(8,128)} %bitcast.6), custom_call_target="tpu_custom_call" | custom-call | flops 3600000000 | bytes 12000000 | tf_op jit(solution)/shard_map/pallas_call | solution.py:451
  102.6 0.0 copy-start
  102.7 0.0 copy-start.1
  102.7 2.7 %copy.12 = bf16[3,256,1024]{2,1,0:T(8,128)(2,1)} copy(bf16[3,256,1024]{2,1,0:T(8,128)(2,1)} %get-tuple-element.12) | data formatting | bytes 3145728
  105.3 0.0 copy-done
  105.3 0.6 copy.13
  105.9 0.0 copy-done.1
  105.9 0.5 copy.14
Async XLA Ops:
  102.6 2.7 %copy-start = (f32[1,1024]{1,0:T(1,128)S(1)}, f32[1,1024]{1,0:T(1,128)}, u32[]{:S(2)}) copy-start(f32[1,1024]{1,0:T(1,128)} %get-tuple-element.7) | copy-start | bytes 12292
  102.7 3.3 %copy-start.1 = (f32[1,16]{1,0:T(1,128)S(1)}, f32[1,16]{1,0:T(1,128)}, u32[]{:S(2)}) copy-start(f32[1,16]{1,0:T(1,128)} %get-tuple-element.8) | copy-start | bytes 196

commit v7 on v6

--- a/solution.py
+++ b/solution.py
@@ -14,8 +14,8 @@
 BF16 = jnp.bfloat16
 MESH = pl.DeviceIdType.MESH
 
-(A1, T1, TG, TY, TX, TX2, T3, TGS, B0, B1, S1, C1, U1, U2, V1, V2, W1, W2, R1, R2, GM, GS, JM, JS) = range(24)
-STAGES = 24
+(A1, T1, TG, TY, TX, TX2, T3, TGS, B0, B1, S1, C1, U1, U2, V1, V2, W1, W2, R1, R2, GM, GS, JM, JS, LX, LY, LXY, LYX) = range(28)
+STAGES = 28
 
 
 def kernel(
@@ -25,7 +25,7 @@
     sq_s, sq_r, mask, lt, ld, placed, grad,
     us1, ur1, us2, ur2, vs1, vr1, vs2, vr2, ws1, wr1, ws2, wr2,
     hf, hb, r0, r1s, r1r, r2s, r2r, gp_s, gp_r, gs_s, gs_r, jg, feat_t, wg,
-    load_sem, ssem, rsem, c2s, c2r, c3s, c3r, r0s, r0r, out_sem,
+    load_sem, ssem, rsem, c2r, c3s, c3r, r0s, r0r, out_sem,
 ):
     d = lax.axis_index("dp")
     c = lax.axis_index("section")
@@ -33,6 +33,8 @@
     z = m // 2
     yh = m % 2
     p = d * 2 + yh
+    px = d // 2
+    py = d % 2 * 2 + yh
     sib = (d, 1 - c, m)
 
     loads = [
@@ -77,8 +79,10 @@
         A1: featg.at[pl.ds(0, 7)], T1: xr.at[c, d, pl.ds(0, 15)], TG: tg.at[c, pl.ds(0, 15)], TY: xr.at[c, d],
         TX: xr.at[c, pl.ds(0, 6), pl.ds(0, 10)],
         TX2: xr.at[c, pl.ds(0, 6), pl.ds(0, 6)], T3: xr.at[c], TGS: tg.at[c], B0: brecv0, B1: bsum.at[pl.ds(0, 15)],
-        S1: sq_r.at[pl.ds(0, 31)], C1: xd.at[c, p, pl.ds(0, 7)], U1: ur1.at[pl.ds(0, 15)], U2: ur2.at[pl.ds(0, 15)],
-        W1: wr1.at[pl.ds(0, 15)], W2: wr2.at[pl.ds(0, 15)], V1: vr1.at[pl.ds(0, 15)], V2: vr2.at[pl.ds(0, 15)], R1: r1r.at[pl.ds(0, 15)], R2: r2r.at[pl.ds(0, 7)],
+        S1: sq_r.at[pl.ds(0, 31)], C1: xd.at[:, c, px, py, pl.ds(0, 7)],
+        LX: xd.at[0, c, pl.ds(0, 3), py], LY: xd.at[1, c, px, pl.ds(0, 3)], LXY: xd.at[0, c, pl.ds(0, 3)], LYX: xd.at[1, c, pl.ds(0, 3)],
+        U1: ur1.at[pl.ds(0, 7)], U2: ur2.at[pl.ds(0, 31)],
+        W1: wr1.at[pl.ds(0, 15)], W2: wr2.at[pl.ds(0, 15)], V1: vr1.at[pl.ds(0, 7)], V2: vr2.at[pl.ds(0, 31)], R1: r1r.at[pl.ds(0, 15)], R2: r2r.at[pl.ds(0, 7)],
         GM: gp_r.at[pl.ds(0, 15)], GS: gs_s, JM: jg.at[c, pl.ds(0, 15)], JS: jg.at[c],
     }
 
@@ -196,8 +200,10 @@
     load_dg.wait()
     own_cols = pl.multiple_of((c * 2 + yh) * 256, 256)
     gain = dgain[:, pl.ds(own_cols, 256)]
-    xd[c, p, z] = (js * dscale * gain).astype(BF16)
-    to_z(xd.at[c, p, z], xd.at[c, p, z], C1)
+    normed = (js * dscale * gain).astype(BF16)
+    xd[0, c, px, py, z] = normed[:, :128]
+    xd[1, c, px, py, z] = normed[:, 128:]
+    to_z(xd.at[:, c, px, py, z], xd.at[:, c, px, py, z], C1)
 
     load_tg.wait()
     arrived(TG)
@@ -205,27 +211,42 @@
 
     arrived(C1)
 
-    def c2(i):
-        q = (p + step(i, 16)) % 16
+    def at_x(i):
+        return ((px + i) % 4 * 2 + d % 2, c, m)
+
+    def at_y(i):
+        k = (py + i) % 4
+        return (px * 2 + k // 2, c, z * 2 + k % 2)
+
+    for i in (1, 3, 2):
+        send(xd.at[0, c, px, py], xd.at[0, c, px, py], LX, at_x(i))
+        send(xd.at[1, c, px, py], xd.at[1, c, px, py], LY, at_y(i))
+
+    def line(half, k):
+        return xd.at[0, c, :, k] if half == 0 else xd.at[1, c, k]
+
+    def second(half, i):
+        own = line(half, (py, px)[half])
         return pltpu.make_async_remote_copy(
-            src_ref=xd.at[c, p], dst_ref=xd.at[c, p], send_sem=c2s, recv_sem=c2r.at[p],
-            device_id=(q // 2, c, z * 2 + q % 2), device_id_type=MESH,
+            src_ref=own, dst_ref=own, send_sem=ssem.at[(LXY, LYX)[half]], recv_sem=c2r.at[half * 4 + (py, px)[half]],
+            device_id=(at_y, at_x)[half](i), device_id_type=MESH,
         )
 
-    def c3(q):
+    def c3(half, k):
         return pltpu.make_async_remote_copy(
-            src_ref=xd.at[c, q], dst_ref=xd.at[c, q], send_sem=c3s, recv_sem=c3r,
+            src_ref=line(half, k), dst_ref=line(half, k), send_sem=c3s, recv_sem=c3r,
             device_id=sib, device_id_type=MESH,
         )
 
-    @pl.loop(1, 16)
-    def _(i):
-        c2(i).start()
-
-    c3(p).start()
     arrived(TX)
     arrived(TX2)
     send(xr.at[c], xr.at[c], T3, sib)
+    for half in range(2):
+        arrived((LX, LY)[half])
+        for i in (1, 3, 2):
+            second(half, i).start()
+    for half in range(2):
+        c3(half, (py, px)[half]).start()
 
     arrived(T3)
     arrived(TGS)
@@ -276,21 +297,23 @@
         return top, zz, ww
 
     us1[...] = rows_of(tmax, tz, tw)
-    to_mp(us1, ur1.at[m], U1)
-    ur1[m] = us1[...]
-
-    @pl.loop(1, 16)
-    def _(i):
-        q = (p + step(i, 16)) % 16
-        pltpu.make_async_copy(xd.at[c, q], xd.at[c, q], c2r.at[q]).wait()
-        c3(q).start()
-
-    pltpu.make_async_copy(xd.at[1 - c], xd.at[1 - c], c3r).wait()
+    to_z(us1, ur1.at[z], U1)
+    ur1[z] = us1[...]
+
+    for i in (1, 3, 2):
+        for half in range(2):
+            k = ((py, px)[half] + i) % 4
+            pltpu.make_async_copy(line(half, k), line(half, k), c2r.at[half * 4 + k]).wait()
+            c3(half, k).start()
+
+    pltpu.make_async_copy(xd.at[:, 1 - c], xd.at[:, 1 - c], c3r).wait()
     ld[...] = jnp.zeros_like(ld)
 
     @pl.loop(0, 8)
     def _(i):
-        x = jnp.concatenate([xd[k // 2, i * 2 + k % 2].reshape(128, 256) for k in range(4)], axis=1)
+        x = jnp.concatenate(
+            [xd[h, k // 2, i // 2, i % 2 * 2 + k % 2].reshape(128, 128) for k in range(4) for h in range(2)], axis=1
+        )
         cols = pl.ds(pl.multiple_of(i * 1024, 1024), 1024)
         ld[...] += lax.dot_general(head[:, cols], x, (((1,), (1,)), ((), ())), preferred_element_type=F32)
 
@@ -301,18 +324,18 @@
     dz = jnp.sum(e, axis=0, keepdims=True)
     ds = jnp.sum(e * away, axis=0, keepdims=True)
     vs1[...] = rows_of(dmax, dz, ds)
-    to_mp(vs1, vr1.at[m], V1)
-    vr1[m] = vs1[...]
+    to_z(vs1, vr1.at[z], V1)
+    vr1[z] = vs1[...]
 
     arrived(U1)
     us2[...] = rows_of(*merge(ur1))
-    to_dp_both(us2, ur2.at[d * 2 + c], U2)
-    ur2[d * 2 + c] = us2[...]
+    to_plane_both(us2, ur2.at[p * 2 + c], U2)
+    ur2[p * 2 + c] = us2[...]
 
     arrived(V1)
     vs2[...] = rows_of(*merge(vr1))
-    to_dp_both(vs2, vr2.at[d * 2 + c], V2)
-    vr2[d * 2 + c] = vs2[...]
+    to_plane_both(vs2, vr2.at[p * 2 + c], V2)
+    vr2[p * 2 + c] = vs2[...]
 
     arrived(U2)
     tmax, tz, tw = merge(ur2)
@@ -438,8 +461,7 @@
 
     for stage in volume:
         sent(stage)
-    pltpu.make_async_copy(xd.at[c, pl.ds(0, 15)], xd.at[c, pl.ds(0, 15)], c2s).wait()
-    pltpu.make_async_copy(xd.at[c], xd.at[c], c3s).wait()
+    pltpu.make_async_copy(xd.at[:, c], xd.at[:, c], c3s).wait()
     pltpu.make_async_copy(r0, r0, r0s).wait()
 
 
@@ -447,7 +469,7 @@
     vmem = pl.BlockSpec(memory_space=pltpu.VMEM)
     hbm = pl.BlockSpec(memory_space=pl.ANY)
     V = pltpu.VMEM
-    stat = [V((4, 128), F32), V((16, 4, 128), F32)] * 2
+    stat = [V((4, 128), F32), V((8, 4, 128), F32), V((4, 128), F32), V((32, 4, 128), F32)]
     weight_grad, gain_grad, loss = pl.pallas_call(
         kernel,
         out_shape=(
@@ -469,7 +491,7 @@
             V((16, 16, 256), F32),
             V((2, 8, 16, 16, 256), BF16),
             V((2, 16, 1, 256), F32),
-            V((2, 16, 8, 16, 256), BF16),
+            V((2, 2, 4, 4, 8, 16, 128), BF16),
             V((16, 256), F32),
             V((1, 128), F32),
             V((32, 1, 128), F32),
@@ -498,8 +520,7 @@
             pltpu.SemaphoreType.DMA((7,)),
             pltpu.SemaphoreType.DMA((STAGES,)),
             pltpu.SemaphoreType.DMA((STAGES,)),
-            pltpu.SemaphoreType.DMA,
-            pltpu.SemaphoreType.DMA((16,)),
+            pltpu.SemaphoreType.DMA((8,)),
             pltpu.SemaphoreType.DMA,
             pltpu.SemaphoreType.DMA,
             pltpu.SemaphoreType.DMA,

time: 107 us -> 103 us (0.963)
  Pallas kernels: 102 us -> 98.5 us
    pallas_call x1, Pallas kernels: 102 us -> 98.5 us  [shards(): pl.pallas_call(kernel, out_shape=(jax.ShapeDtypeStruct((3, 256, 1024), BF...]
where the time goes in v7:
time: 103 us
  Pallas kernels  98.5 us (96%)
  local copies, waits for them, and re-layouts  3.78 us (4%)
    pallas_call x1, Pallas kernels, shards(): pl.pallas_call(kernel, out_shape=(jax.ShapeDtypeStruct((3, 256, 1024), BF...  98.5 us
    unnamed x7, local copies, waits for them, and re-layouts  3.78 us

profile of v7, /device:TPU:1, one launch (start us, length us, event | category | flops | bytes accessed | tf_op | source)
XLA Modules:
  0.0 103.0 jit_solution(8879249551820958712)
XLA Ops:
  0.6 98.5 %shard_map.85 = (bf16[3,256,1024]{2,1,0:T(8,128)(2,1)}, f32[1,1024]{1,0:T(1,128)}, f32[1,16]{1,0:T(1,128)}) custom-call(bf16[3,16,256]{2,1,0:T(8,128)(2,1)} %feat.1, bf16[3,256,1024]{2,1,0:T(8,128)(2,1)} %fc_hbm.1, bf16[501,8192]{1,0:T(8,128)(2,1)} %head_hbm.1, f32[1,1024]{1,0:T(1,128)} %bitcast.7, f32[1,256]{1,0:T(1,128)} %bitcast.8, s32[32,128]{1,0:T(8,128)} %bitcast.6), custom_call_target="tpu_custom_call" | custom-call | flops 3600000000 | bytes 12000000 | tf_op jit(solution)/shard_map/pallas_call | solution.py:473
  99.2 0.0 copy-start
  99.2 0.0 copy-start.1
  99.2 2.7 %copy.12 = bf16[3,256,1024]{2,1,0:T(8,128)(2,1)} copy(bf16[3,256,1024]{2,1,0:T(8,128)(2,1)} %get-tuple-element.12) | data formatting | bytes 3145728
  101.8 0.0 copy-done
  101.8 0.6 copy.13
  102.4 0.0 copy-done.1
  102.4 0.5 copy.14
Async XLA Ops:
  99.2 2.7 %copy-start = (f32[1,1024]{1,0:T(1,128)S(1)}, f32[1,1024]{1,0:T(1,128)}, u32[]{:S(2)}) copy-start(f32[1,1024]{1,0:T(1,128)} %get-tuple-element.7) | copy-start | bytes 12292
  99.2 3.3 %copy-start.1 = (f32[1,16]{1,0:T(1,128)S(1)}, f32[1,16]{1,0:T(1,128)}, u32[]{:S(2)}) copy-start(f32[1,16]{1,0:T(1,128)} %get-tuple-element.8) | copy-start | bytes 196

commit v8 on v7

--- a/solution.py
+++ b/solution.py
@@ -14,8 +14,8 @@
 BF16 = jnp.bfloat16
 MESH = pl.DeviceIdType.MESH
 
-(A1, T1, TG, TY, TX, TX2, T3, TGS, B0, B1, S1, C1, U1, U2, V1, V2, W1, W2, R1, R2, GM, GS, JM, JS, LX, LY, LXY, LYX) = range(28)
-STAGES = 28
+(A1, T1, TG, TY, TX, TX2, T3, TGS, B0, B1, S1, C1, U1, U2, V1, V2, W1, W2, RY, RX, RYX, RXY, R2, GM, GS, JM, JS, LX, LY, LXY, LYX) = range(31)
+STAGES = 31
 
 
 def kernel(
@@ -24,7 +24,7 @@
     head, fc, featg, dgain, index, part, brecv0, bsum, brecv1, xr, tg, xd, joined,
     sq_s, sq_r, mask, lt, ld, placed, grad,
     us1, ur1, us2, ur2, vs1, vr1, vs2, vr2, ws1, wr1, ws2, wr2,
-    hf, hb, r0, r1s, r1r, r2s, r2r, gp_s, gp_r, gs_s, gs_r, jg, feat_t, wg,
+    hf, hb, r0, r1s, ra, rb_s, rb_r, r2s, r2r, gp_s, gp_r, gs_s, gs_r, jg, feat_t, wg,
     load_sem, ssem, rsem, c2r, c3s, c3r, r0s, r0r, out_sem,
 ):
     d = lax.axis_index("dp")
@@ -82,7 +82,8 @@
         S1: sq_r.at[pl.ds(0, 31)], C1: xd.at[:, c, px, py, pl.ds(0, 7)],
         LX: xd.at[0, c, pl.ds(0, 3), py], LY: xd.at[1, c, px, pl.ds(0, 3)], LXY: xd.at[0, c, pl.ds(0, 3)], LYX: xd.at[1, c, pl.ds(0, 3)],
         U1: ur1.at[pl.ds(0, 7)], U2: ur2.at[pl.ds(0, 31)],
-        W1: wr1.at[pl.ds(0, 15)], W2: wr2.at[pl.ds(0, 15)], V1: vr1.at[pl.ds(0, 7)], V2: vr2.at[pl.ds(0, 31)], R1: r1r.at[pl.ds(0, 15)], R2: r2r.at[pl.ds(0, 7)],
+        W1: wr1.at[pl.ds(0, 15)], W2: wr2.at[pl.ds(0, 15)], V1: vr1.at[pl.ds(0, 7)], V2: vr2.at[pl.ds(0, 31)], RY: ra.at[0, pl.ds(0, 3)], RX: ra.at[1, pl.ds(0, 3)],
+        RYX: rb_r.at[0, pl.ds(0, 3)], RXY: rb_r.at[1, pl.ds(0, 3)], R2: r2r.at[pl.ds(0, 7)],
         GM: gp_r.at[pl.ds(0, 15)], GS: gs_s, JM: jg.at[c, pl.ds(0, 15)], JS: jg.at[c],
     }
 
@@ -372,10 +373,22 @@
         pltpu.make_async_copy(r0.at[pl.ds(dd * 2, 2)], r0.at[pl.ds(dd * 2, 2)], r0r.at[dd]).wait()
         for k in range(2):
             q = dd * 2 + k
-            r1s[q] = (hf[c, q] + r0[q].astype(F32)).astype(BF16)
-
-    def to_peer(q):
-        send(r1s.at[q], r1r.at[p], R1, (q // 2, c, z * 2 + q % 2))
+            total = (hf[c, q] + r0[q].astype(F32)).astype(BF16)
+            r1s[0, dd // 2, dd % 2 * 2 + k] = total[:, :128]
+            r1s[1, dd // 2, dd % 2 * 2 + k] = total[:, 128:]
+
+    def to_lines(dd):
+        x = dd // 2
+        for k in range(2):
+            y = dd % 2 * 2 + k
+
+            @pl.when(y != py)
+            def _():
+                send(r1s.at[0, x, y], ra.at[0, py, x], RY, (px * 2 + y // 2, c, z * 2 + k))
+
+            @pl.when(x != px)
+            def _():
+                send(r1s.at[1, x, y], ra.at[1, px, y], RX, (x * 2 + d % 2, c, m))
 
     compute((d + 1) % 8)
 
@@ -384,22 +397,35 @@
         compute((d + step(i, 8) * (1 - i // 8)) % 8)
         dd = (d + step(i - 1, 8)) % 8
         add_up(dd)
-        to_peer(dd * 2)
-        to_peer(dd * 2 + 1)
+        to_lines(dd)
 
     add_up(d)
-    to_peer(d * 2 + 1 - yh)
-    r1r[p] = r1s[p]
+    to_lines(d)
+    ra[0, py] = r1s[0, :, py]
+    ra[1, px] = r1s[1, px]
     arrived(W1)
     ws2[...] = jnp.sum(wr1[...], axis=0)
     to_dp_both(ws2, wr2.at[d * 2 + c], W2)
     wr2[d * 2 + c] = ws2[...]
-    arrived(R1)
-    for zz in range(8):
-        acc = r1r[0, zz * 16 : zz * 16 + 16].astype(F32)
-        for k in range(1, 16):
-            acc += r1r[k, zz * 16 : zz * 16 + 16].astype(F32)
-        r2s[zz] = acc.astype(BF16)
+    for half in range(2):
+        arrived((RY, RX)[half])
+        for k in range(4):
+            acc = ra[half, 0, k].astype(F32)
+            for i in range(1, 4):
+                acc += ra[half, i, k].astype(F32)
+            rb_s[half, k] = acc.astype(BF16)
+        own = (px, py)[half]
+        for i in (1, 3, 2):
+            send(rb_s.at[half, (own + i) % 4], rb_r.at[half, own], (RYX, RXY)[half], (at_x, at_y)[half](i))
+        rb_r[half, own] = rb_s[half, own]
+    for half in range(2):
+        arrived((RYX, RXY)[half])
+        for zz in range(8):
+            rows = slice(zz * 16, zz * 16 + 16)
+            acc = rb_r[half, 0, rows].astype(F32)
+            for i in range(1, 4):
+                acc += rb_r[half, i, rows].astype(F32)
+            r2s[zz, :, half * 128 : half * 128 + 128] = acc.astype(BF16)
 
     @pl.loop(1, 8)
     def _(i):
@@ -506,8 +532,10 @@
             V((2, 16, 128, 256), F32),
             V((2, 16, 128, 256), BF16),
             V((16, 128, 256), BF16),
-            V((16, 128, 256), BF16),
-            V((16, 128, 256), BF16),
+            V((2, 4, 4, 128, 128), BF16),
+            V((2, 4, 4, 128, 128), BF16),
+            V((2, 4, 128, 128), BF16),
+            V((2, 4, 128, 128), BF16),
             V((8, 16, 256), BF16),
             V((8, 16, 256), BF16),
             V((1, 256), F32),

time: 103 us -> 100 us (0.971)
  Pallas kernels: 98.5 us -> 95.7 us
    pallas_call x1, Pallas kernels: 98.5 us -> 95.7 us  [shards(): pl.pallas_call(kernel, out_shape=(jax.ShapeDtypeStruct((3, 256, 1024), BF...]
where the time goes in v8:
time: 100 us
  Pallas kernels  95.7 us (96%)
  local copies, waits for them, and re-layouts  3.78 us (4%)
    pallas_call x1, Pallas kernels, shards(): pl.pallas_call(kernel, out_shape=(jax.ShapeDtypeStruct((3, 256, 1024), BF...  95.7 us
    unnamed x7, local copies, waits for them, and re-layouts  3.78 us

profile of v8, /device:TPU:1, one launch (start us, length us, event | category | flops | bytes accessed | tf_op | source)
XLA Modules:
  0.0 100.1 jit_solution(12951267813690749573)
XLA Ops:
  0.6 95.7 %shard_map.85 = (bf16[3,256,1024]{2,1,0:T(8,128)(2,1)}, f32[1,1024]{1,0:T(1,128)}, f32[1,16]{1,0:T(1,128)}) custom-call(bf16[3,16,256]{2,1,0:T(8,128)(2,1)} %feat.1, bf16[3,256,1024]{2,1,0:T(8,128)(2,1)} %fc_hbm.1, bf16[501,8192]{1,0:T(8,128)(2,1)} %head_hbm.1, f32[1,1024]{1,0:T(1,128)} %bitcast.7, f32[1,256]{1,0:T(1,128)} %bitcast.8, s32[32,128]{1,0:T(8,128)} %bitcast.6), custom_call_target="tpu_custom_call" | custom-call | flops 3600000000 | bytes 12000000 | tf_op jit(solution)/shard_map/pallas_call | solution.py:499
  96.3 0.0 copy-start
  96.3 0.0 copy-start.1
  96.4 2.7 %copy.12 = bf16[3,256,1024]{2,1,0:T(8,128)(2,1)} copy(bf16[3,256,1024]{2,1,0:T(8,128)(2,1)} %get-tuple-element.12) | data formatting | bytes 3145728
  99.0 0.0 copy-done
  99.0 0.6 copy.13
  99.6 0.0 copy-done.1
  99.6 0.5 copy.14
Async XLA Ops:
  96.3 2.7 %copy-start = (f32[1,1024]{1,0:T(1,128)S(1)}, f32[1,1024]{1,0:T(1,128)}, u32[]{:S(2)}) copy-start(f32[1,1024]{1,0:T(1,128)} %get-tuple-element.7) | copy-start | bytes 12292
  96.3 3.3 %copy-start.1 = (f32[1,16]{1,0:T(1,128)S(1)}, f32[1,16]{1,0:T(1,128)}, u32[]{:S(2)}) copy-start(f32[1,16]{1,0:T(1,128)} %get-tuple-element.8) | copy-start | bytes 196

commit v9 on v8

--- a/solution.py
+++ b/solution.py
@@ -14,8 +14,8 @@
 BF16 = jnp.bfloat16
 MESH = pl.DeviceIdType.MESH
 
-(A1, T1, TG, TY, TX, TX2, T3, TGS, B0, B1, S1, C1, U1, U2, V1, V2, W1, W2, RY, RX, RYX, RXY, R2, GM, GS, JM, JS, LX, LY, LXY, LYX) = range(31)
-STAGES = 31
+(A1, T1, TG, TY, TX, TX2, T3, TGS, B0, B1, S1, C1, U1, U2, V1, V2, W1, W2, RY, RX, RYX, RXY, R2, GM, GS, JM, JS, LX, LY, LXY, LYX, T3B) = range(32)
+STAGES = 32
 
 
 def kernel(
@@ -78,7 +78,7 @@
     volume = {
         A1: featg.at[pl.ds(0, 7)], T1: xr.at[c, d, pl.ds(0, 15)], TG: tg.at[c, pl.ds(0, 15)], TY: xr.at[c, d],
         TX: xr.at[c, pl.ds(0, 6), pl.ds(0, 10)],
-        TX2: xr.at[c, pl.ds(0, 6), pl.ds(0, 6)], T3: xr.at[c], TGS: tg.at[c], B0: brecv0, B1: bsum.at[pl.ds(0, 15)],
+        TX2: xr.at[c, pl.ds(0, 6), pl.ds(0, 6)], T3: xr.at[c, :, pl.ds(0, 10)], T3B: xr.at[c, :, pl.ds(10, 6)], TGS: tg.at[c], B0: brecv0, B1: bsum.at[pl.ds(0, 15)],
         S1: sq_r.at[pl.ds(0, 31)], C1: xd.at[:, c, px, py, pl.ds(0, 7)],
         LX: xd.at[0, c, pl.ds(0, 3), py], LY: xd.at[1, c, px, pl.ds(0, 3)], LXY: xd.at[0, c, pl.ds(0, 3)], LYX: xd.at[1, c, pl.ds(0, 3)],
         U1: ur1.at[pl.ds(0, 7)], U2: ur2.at[pl.ds(0, 31)],
@@ -209,6 +209,8 @@
     load_tg.wait()
     arrived(TG)
     send(tg.at[c], tg.at[c], TGS, sib)
+    arrived(TX)
+    send(xr.at[c, :, pl.ds(0, 10)], xr.at[c, :, pl.ds(0, 10)], T3, sib)
 
     arrived(C1)
 
@@ -239,9 +241,8 @@
             device_id=sib, device_id_type=MESH,
         )
 
-    arrived(TX)
     arrived(TX2)
-    send(xr.at[c], xr.at[c], T3, sib)
+    send(xr.at[c, :, pl.ds(10, 6)], xr.at[c, :, pl.ds(10, 6)], T3B, sib)
     for half in range(2):
         arrived((LX, LY)[half])
         for i in (1, 3, 2):
@@ -250,6 +251,7 @@
         c3(half, (py, px)[half]).start()
 
     arrived(T3)
+    arrived(T3B)
     arrived(TGS)
 
     def add_squares(i, acc):

time: 100 us -> 100 us (level)
  no operation moved by 1% of the time
where the time goes in v9:
time: 100 us
  Pallas kernels  95.7 us (96%)
  local copies, waits for them, and re-layouts  3.78 us (4%)
    pallas_call x1, Pallas kernels, shards(): pl.pallas_call(kernel, out_shape=(jax.ShapeDtypeStruct((3, 256, 1024), BF...  95.7 us
    unnamed x7, local copies, waits for them, and re-layouts  3.78 us

profile of v9, /device:TPU:1, one launch (start us, length us, event | category | flops | bytes accessed | tf_op | source)
XLA Modules:
  0.0 100.2 jit_solution(14066228767074240250)
XLA Ops:
  0.6 95.7 %shard_map.85 = (bf16[3,256,1024]{2,1,0:T(8,128)(2,1)}, f32[1,1024]{1,0:T(1,128)}, f32[1,16]{1,0:T(1,128)}) custom-call(bf16[3,16,256]{2,1,0:T(8,128)(2,1)} %feat.1, bf16[3,256,1024]{2,1,0:T(8,128)(2,1)} %fc_hbm.1, bf16[501,8192]{1,0:T(8,128)(2,1)} %head_hbm.1, f32[1,1024]{1,0:T(1,128)} %bitcast.7, f32[1,256]{1,0:T(1,128)} %bitcast.8, s32[32,128]{1,0:T(8,128)} %bitcast.6), custom_call_target="tpu_custom_call" | custom-call | flops 3600000000 | bytes 12000000 | tf_op jit(solution)/shard_map/pallas_call | solution.py:501
  96.4 0.0 copy-start
  96.4 0.0 copy-start.1
  96.4 2.7 %copy.12 = bf16[3,256,1024]{2,1,0:T(8,128)(2,1)} copy(bf16[3,256,1024]{2,1,0:T(8,128)(2,1)} %get-tuple-element.12) | data formatting | bytes 3145728
  99.0 0.0 copy-done
  99.0 0.6 copy.13
  99.6 0.0 copy-done.1
  99.6 0.5 copy.14
Async XLA Ops:
  96.4 2.7 %copy-start = (f32[1,1024]{1,0:T(1,128)S(1)}, f32[1,1024]{1,0:T(1,128)}, u32[]{:S(2)}) copy-start(f32[1,1024]{1,0:T(1,128)} %get-tuple-element.7) | copy-start | bytes 12292
  96.4 3.3 %copy-start.1 = (f32[1,16]{1,0:T(1,128)S(1)}, f32[1,16]{1,0:T(1,128)}, u32[]{:S(2)}) copy-start(f32[1,16]{1,0:T(1,128)} %get-tuple-element.8) | copy-start | bytes 196
